TPU v7x, 128 devices: a whole 4x4x4 slice. The times are simulated.
128 devices in a mesh: pool: 4 (over z_lo, core), dev: 32 (over x, y, z_hi).
Axes of the slice: x: 4, y: 4, z: 4 (z_hi: 2, z_lo: 2; z = z_hi * 2 + z_lo), core: 2. Of those that a mesh axis runs over, the one named last changes fastest.
Arguments:
- hidden_in: bfloat16 [32, 7168], P('pool', 'dev'), may hold values from -32 to 32
- in_gain: float32 [7168], P('dev'), may hold values from 0.25 to 1.75
- w_latent: bfloat16 [7168, 2560], P('dev'), may hold values from -0.0625 to 0.0625
- q_gain: float32 [2048], replicated, may hold values from 0.25 to 1.75
- w_query: bfloat16 [2048, 16384], P(None, 'dev'), may hold values from -0.125 to 0.125
- cache_keys: bfloat16 [32, 16384, 256], P('pool', 'dev'), may hold values from -240 to 240
- cache_values: bfloat16 [32, 16384, 256], P('pool', 'dev'), may hold values from -6 to 6
- lengths: int32 [32], P('pool'), may hold values from 1 to 16384, 262144 in all
- w_out: bfloat16 [16384, 7168], P('dev'), may hold values from -0.1875 to 0.1875
- post_gain: float32 [7168], P('dev'), may hold values from 0.25 to 1.75
- w_gate: bfloat16 [7168, 18432], P(None, ('pool', 'dev')), may hold values from -0.0625 to 0.0625
- w_up: bfloat16 [7168, 18432], P(None, ('pool', 'dev')), may hold values from -0.0625 to 0.0625
- w_down: bfloat16 [18432, 7168], P(('pool', 'dev')), may hold values from -0.15625 to 0.15625
Outputs:
- mixed: float32 [32, 7168], P('pool', 'dev')
All inputs are finite; a program needn't handle non-finite values. No bound on the sum of `lengths` on one device may be relied on, other than what follows from the above.
Results may differ from a plain program's by a relative error of at most 0.013.
Values may be sent and summed in bfloat16 or wider, within the bound.
A program may use at most 128 MiB of HBM per device.

v0:
```python
import math

import jax
import jax.numpy as jnp
from jax import lax
from jax.sharding import PartitionSpec as P

D = 7168
H = 64
HD = 256
QR = 2048


EPS = 1e-05
NEG = -1e30


def merged(value, axis, join):
    pieces = jax.tree.map(lambda part: lax.all_gather(part, axis), value)
    head = jax.tree.map(lambda part: part[0], pieces)
    tail = jax.tree.map(lambda part: part[1:], pieces)
    so_far, _ = lax.scan(lambda so_far, section: (join(so_far, section), None), head, tail)
    return so_far


def combine_parts(left_part, right_part):
    highest = jnp.maximum(left_part[0], right_part[0])
    left_factor = jnp.exp(left_part[0] - highest)
    right_factor = jnp.exp(right_part[0] - highest)
    mass = left_part[1] * left_factor + right_part[1] * right_factor
    summed = left_part[2] * left_factor[..., None] + right_part[2] * right_factor[..., None]
    return (highest, mass, summed)


def local(
    hidden_in,
    in_gain,
    w_latent,
    q_gain,
    w_query,
    cache_keys,
    cache_values,
    lengths,
    w_out,
    post_gain,
    w_gate,
    w_up,
    w_down,
):
    n_dev = lax.axis_size("dev")
    n_pool = lax.axis_size("pool")
    rows_here = hidden_in.shape[0]
    local_pos = cache_keys.shape[1]
    head_cols = w_out.shape[0]
    scale_inv = 1.0 / math.sqrt(HD)
    hidden_f = hidden_in.astype(jnp.float32)
    scaled_in = (hidden_f * in_gain[None, :]).astype(jnp.bfloat16)
    latent_part = jnp.dot(scaled_in, w_latent, preferred_element_type=jnp.float32)
    square_part = jnp.sum(hidden_f * hidden_f, axis=1)
    latent, squares = lax.psum((latent_part, square_part), "dev")
    latent = latent * lax.rsqrt(squares / D + EPS)[:, None]
    query_latent = latent[:, :QR]
    key_new = latent[:, QR : QR + HD].astype(jnp.bfloat16)
    value_new = latent[:, QR + HD :].astype(jnp.bfloat16)
    latent_mean = jnp.mean(query_latent * query_latent, axis=1)
    query_normed = (query_latent * lax.rsqrt(latent_mean + EPS)[:, None] * q_gain[None, :]).astype(
        jnp.bfloat16
    )
    query_local = jnp.dot(query_normed, w_query, preferred_element_type=jnp.float32).astype(
        jnp.bfloat16
    )
    query_all = lax.all_gather(query_local, "dev", axis=1, tiled=True).reshape(rows_here, H, HD)
    scores = (
        jnp.einsum("rhd,rpd->rhp", query_all, cache_keys, preferred_element_type=jnp.float32)
        * scale_inv
    )
    positions = lax.axis_index("dev") * local_pos + jnp.arange(local_pos, dtype=jnp.int32)
    valid_mask = (positions[None, :] < lengths[:, None])[:, None, :]
    masked = jnp.where(valid_mask, scores, NEG)
    top_local = jnp.max(masked, axis=-1)
    weights = jnp.where(valid_mask, jnp.exp(masked - top_local[..., None]), 0.0)
    mass_local = jnp.sum(weights, axis=-1)
    weighted = jnp.einsum(
        "rhp,rpd->rhd",
        weights.astype(jnp.bfloat16),
        cache_values,
        preferred_element_type=jnp.float32,
    )
    score_new = (
        jnp.sum(query_all.astype(jnp.float32) * key_new.astype(jnp.float32)[:, None, :], axis=-1)
        * scale_inv
    )
    value_wide = value_new.astype(jnp.float32)[:, None, :]
    own_start = lax.axis_index("dev") * head_cols
    top_all, mass_all, weighted_all = merged(
        (top_local, mass_local, weighted), "dev", combine_parts
    )
    top_new = jnp.maximum(top_all, score_new)
    keep_factor = jnp.exp(top_all - top_new)
    fresh_weight = jnp.exp(score_new - top_new)
    mass_total = mass_all * keep_factor + fresh_weight
    numerator = (
        weighted_all * keep_factor[..., None]
        + fresh_weight.astype(jnp.bfloat16).astype(jnp.float32)[..., None] * value_wide
    )
    attended = (numerator / mass_total[..., None]).astype(jnp.bfloat16).reshape(rows_here, H * HD)
    own_heads = lax.dynamic_slice_in_dim(attended, own_start, head_cols, 1)
    head_sum = jnp.dot(own_heads, w_out, preferred_element_type=jnp.float32)
    attn_part = lax.psum_scatter(head_sum, "dev", scatter_dimension=1, tiled=True)
    residual = hidden_f + attn_part
    row_squares = lax.psum(jnp.sum(residual * residual, axis=1), "dev")
    normed = (residual * lax.rsqrt(row_squares / D + EPS)[:, None] * post_gain[None, :]).astype(
        jnp.bfloat16
    )
    slice_cols = normed.shape[1]
    ff_cols = w_gate.shape[1]
    gathered = lax.all_gather(normed, ("pool", "dev"), axis=0, tiled=True).reshape(
        n_pool, n_dev, rows_here, slice_cols
    )
    gate_out = jnp.einsum(
        "pdrc,dcf->prf",
        gathered,
        w_gate.reshape(n_dev, slice_cols, ff_cols),
        preferred_element_type=jnp.float32,
    )
    up_out = jnp.einsum(
        "pdrc,dcf->prf",
        gathered,
        w_up.reshape(n_dev, slice_cols, ff_cols),
        preferred_element_type=jnp.float32,
    )
    activated = (jax.nn.silu(gate_out) * up_out).astype(jnp.bfloat16)
    ffn_term = jnp.einsum(
        "prf,fdc->pdrc",
        activated,
        w_down.reshape(ff_cols, n_dev, slice_cols),
        preferred_element_type=jnp.float32,
    )
    ffn_term = ffn_term.reshape(n_pool * n_dev * rows_here, slice_cols)
    ffn_out = lax.psum_scatter(ffn_term, ("pool", "dev"), scatter_dimension=0, tiled=True)
    return residual + ffn_out


def solution(mesh):
    placed = (
        P("pool", "dev"),
        P("dev"),
        P("dev", None),
        P(),
        P(None, "dev"),
        P("pool", "dev", None),
        P("pool", "dev", None),
        P("pool"),
        P("dev", None),
        P("dev"),
        P(None, ("pool", "dev")),
        P(None, ("pool", "dev")),
        P(("pool", "dev"), None),
    )
    return jax.shard_map(
        local, mesh=mesh, in_specs=placed, out_specs=P("pool", "dev"), check_vma=False
    )
```

profile of v0, /device:TPU:0, one launch (start us, length us, event | category | flops | bytes accessed | tf_op | source)
XLA Modules:
  0.0 1945.2 jit_solution(17838719854238407472)
XLA Ops:
  6.5 2.3 fusion.52
  9.7 97.4 %psum.22 = f32[8]{0:T(128)S(1)} all-reduce(f32[8]{0:T(128)S(1)} %fusion.48), channel_id=1, replica_groups=mesh['pool'=4,'dev'=32] {'dev'}, use_global_device_ids=true, to_apply=%region_2.0 | all-reduce | flops 8 | bytes 64 | tf_op jit(solution)/shard_map/psum | solution.py:60
  107.9 222.2 %all-reduce.2.cloned.1.call-done = f32[8,2560]{1,0:T(8,128)} async-done(((f32[8,2560]{1,0:T(8,128)}), f32[8,2560]{1,0:T(8,128)}) %all-reduce.2.cloned.1.call-update) | async-done | bytes 81936 | tf_op jit(solution)/shard_map/psum | solution.py:60
  331.2 2.0 convolution_convert_fusion
  333.3 93.5 %all_gather.24 = bf16[8,16384]{1,0:T(8,128)(2,1)S(1)} all-gather(bf16[8,512]{1,0:T(8,128)(2,1)S(1)} %convolution_convert_fusion), channel_id=1, replica_groups=mesh['pool'=4,'dev'=32] {'dev'}, dimensions={1}, use_global_device_ids=true | all-gather | bytes 270336 | tf_op jit(solution)/shard_map/all_gather | solution.py:72
  427.6 1.4 fusion.32
  429.3 89.0 %all-gather = f32[256,64]{1,0:T(8,128)S(1)} all-gather(f32[8,64]{1,0:T(8,128)S(1)} %get-tuple-element.72), channel_id=2, replica_groups=mesh['pool'=4,'dev'=32] {'dev'}, dimensions={0}, use_global_device_ids=true | all-gather | bytes 67584 | tf_op jit(solution)/shard_map/all_gather | solution.py:19
  518.7 92.3 %all-gather.1 = f32[256,64]{1,0:T(8,128)S(1)} all-gather(f32[8,64]{1,0:T(8,128)S(1)} %fusion.31), channel_id=3, replica_groups=mesh['pool'=4,'dev'=32] {'dev'}, dimensions={0}, use_global_device_ids=true | all-gather | bytes 67584 | tf_op jit(solution)/shard_map/all_gather | solution.py:19
  611.0 11.5 slice.50
  622.5 41.2 %while.14 = (s32[]{:T(128)}, f32[8,64]{1,0:T(8,128)S(1)}, f32[8,64]{1,0:T(8,128)S(1)}, f32[8,64,256]{2,1,0:T(8,128)S(1)}, f32[31,8,64]{2,1,0:T(8,128)S(1)}, /*in...) while((s32[]{:T(128)}, f32[8,64]{1,0:T(8,128)S(1)}, f32[8,64]{1,0:T(8,128)S(1)}, ...), condition=%wide.region_7.8_spmd, body=%wide.region_6.7_spmd.sunk | while | flops 396290 | bytes 1593445 | solution.py:22
  622.6 1.3 fusion.72
  623.9 1.3 fusion.72
  625.2 1.3 fusion.72
  626.5 1.3 fusion.72
  642.5 1.3 fusion.72
  645.2 1.3 fusion.72
  651.8 1.3 fusion.72
  653.1 1.3 fusion.72
  654.5 1.3 fusion.72
  661.1 1.3 fusion.72
  664.2 7.8 convolution_bitcast_fusion
  672.1 1.5 copy-done.3
  673.6 4.2 reshape.69
  677.9 5.8 reshape.70
  683.7 173.7 %reduce-scatter.7.cloned.1.call-done = f32[224,8]{1,0:T(8,128)} async-done(((f32[7168,8]{1,0:T(8,128)}), f32[224,8]{1,0:T(8,128)}) %reduce-scatter.7.cloned.1.call-update) | async-done | bytes 7184
  858.5 4.3 reshape.71
  862.8 89.5 %psum.23 = f32[8]{0:T(128)S(1)} all-reduce(f32[8]{0:T(128)S(1)} %multiply_reduce_fusion.2), channel_id=1, replica_groups=mesh['pool'=4,'dev'=32] {'dev'}, use_global_device_ids=true, to_apply=%region_11.12 | all-reduce | flops 8 | bytes 64 | tf_op jit(solution)/shard_map/psum | solution.py:111
  952.4 324.7 %all_gather.31 = bf16[1024,224]{1,0:T(8,128)(2,1)S(1)} all-gather(bf16[8,224]{1,0:T(8,128)(2,1)S(1)} %multiply_convert_fusion.2), channel_id=1, replica_groups=mesh['pool'=4,'dev'=32] {'pool','dev'}, dimensions={0}, use_global_device_ids=true | all-gather | bytes 462336 | tf_op jit(solution)/shard_map/all_gather | solution.py:117
  1277.2 4.4 fusion.13
  1281.6 8.4 fusion.3
  1290.0 647.3 %reduce-scatter.5.cloned.1.call-done = f32[8,224]{1,0:T(8,128)} async-done(((f32[1024,224]{1,0:T(8,128)}), f32[8,224]{1,0:T(8,128)}) %reduce-scatter.5.cloned.1.call-update) | async-done | bytes 7184 | tf_op jit(solution)/shard_map/reduce_scatter | solution.py:140
  1937.4 1.3 fusion.55
  (99 shorter events, 33.5 us)
Async XLA Ops:
  6.5 420.2 %copy-start = (bf16[8,512,256]{2,1,0:T(8,128)(2,1)S(1)}, bf16[8,512,256]{2,1,0:T(8,128)(2,1)}, u32[]{:S(2)}) copy-start(bf16[8,512,256]{2,1,0:T(8,128)(2,1)} %param.20) | copy-start | bytes 6291460
  6.5 323.6 %all-reduce.2.cloned.1.call-start = ((), (), s32[]{:S(2)}) async-start(), calls=%async_computation.2 | async-start | bytes 163840 | tf_op jit(solution)/shard_map/psum | solution.py:60
  8.9 602.1 %all-gather.5.cloned.1.call-start = ((), (), s32[]{:S(2)}) async-start(), calls=%async_computation.4 | async-start | bytes 17301504 | tf_op jit(solution)/shard_map/all_gather | solution.py:19
  333.3 94.3 %copy-start.2 = (bf16[8,512,256]{2,1,0:T(8,128)(2,1)S(1)}, bf16[8,512,256]{2,1,0:T(8,128)(2,1)}, u32[]{:S(2)}) copy-start(bf16[8,512,256]{2,1,0:T(8,128)(2,1)} %param.21) | copy-start | bytes 6291460
  429.0 428.5 %reduce-scatter.7.cloned.1.call-start = ((), (), s32[]{:S(2)}) async-start(), calls=%async_computation.5 | async-start | bytes 3784704
  611.0 11.5 slice-start
  672.1 1.6 copy-start.3
  672.1 1265.3 %reduce-scatter.5.cloned.1.call-start = ((), (), s32[]{:S(2)}) async-start(), calls=%async_computation.3 | async-start | bytes 1056768 | tf_op jit(solution)/shard_map/reduce_scatter | solution.py:140
  677.9 180.5 %copy-start.5 = (bf16[8,224]{1,0:T(8,128)(2,1)S(1)}, bf16[8,224]{1,0:T(8,128)(2,1)}, u32[]{:S(2)}) copy-start(bf16[8,224]{1,0:T(8,128)(2,1)} %param.15) | copy-start | bytes 10756
  677.9 180.7 %copy-start.4 = (bf16[144,7168]{1,0:T(8,128)(2,1)S(1)}, bf16[144,7168]{1,0:T(8,128)(2,1)}, u32[]{:S(2)}) copy-start(bf16[144,7168]{1,0:T(8,128)(2,1)} %param.27) | copy-start | bytes 6193156
  683.7 268.6 %copy-start.6 = (f32[224]{0:T(256)S(1)}, f32[224]{0:T(256)}, u32[]{:S(2)}) copy-start(f32[224]{0:T(256)} %param.24) | copy-start | bytes 2692
  1277.2 661.5 %copy-start.1 = (bf16[8,512,256]{2,1,0:T(8,128)(2,1)S(1)}, bf16[8,512,256]{2,1,0:T(8,128)(2,1)}, u32[]{:S(2)}) copy-start(bf16[8,512,256]{2,1,0:T(8,128)(2,1)} %param.20) | copy-start | bytes 6291460
Sparse Core Ops, SparseCore 0:
  9.8 320.2 all-reduce.1
  429.1 152.6 all-gather.4
  672.2 185.1 reduce-scatter.6
  1290.2 647.1 reduce-scatter.4
where the time goes:
time: 1950 us
  waiting for transfers between devices  1040 us (53%)
  blocking collectives  787 us (40%)
  other arithmetic  45.4 us (2%)
  local copies, waits for them, and re-layouts  28.6 us (1%)
  matrix products  27.2 us (1%)
    reduce_scatter x1, waiting for transfers between devices, local(): lax.psum_scatter(ffn_term, ('pool', 'dev'), scatter_dimension=0, tiled=True)  647 us
    all_gather x1, blocking collectives, local(): lax.all_gather(normed, ('pool', 'dev'), axis=0, tiled=True)  325 us
    psum x1, waiting for transfers between devices, local(): latent, squares = lax.psum((latent_part, square_part), 'dev')  222 us
    all_gather x2, blocking collectives, merged(): pieces = jax.tree.map(lambda part: lax.all_gather(part, axis), value)  181 us
    unnamed x5, waiting for transfers between devices  174 us
    psum x1, blocking collectives, local(): latent, squares = lax.psum((latent_part, square_part), 'dev')  97.4 us
    all_gather x1, blocking collectives, local(): lax.all_gather(query_local, 'dev', axis=1, tiled=True)  93.5 us
    psum x1, blocking collectives, local(): row_squares = lax.psum(jnp.sum(residual * residual, axis=1), 'dev')  89.5 us
  transfers between devices with their start and end apart: 4, of which 3 were waited for; matrix products, arithmetic and copies ran while one was open for 1% of the time, Pallas kernels for 0%

commit v1 on v0

v1 whole, which is shorter than its diff:
```python
import math

import jax
import jax.numpy as jnp
from jax import lax
from jax.experimental import pallas as pl
from jax.experimental.pallas import tpu as pltpu
from jax.sharding import PartitionSpec as P

D = 7168
H = 64
HD = 256
QR = 2048
EPS = 1e-05
NEG = -1e30
MESH = pl.DeviceIdType.MESH

N_POOL = 4
N_DEV = 32
N_ALL = N_POOL * N_DEV
ROWS = 8
COLS = 224
LANES = 128
CHUNKS = (QR + 2 * HD) // LANES + 1
GROUP = 4
GROUP_COLS = GROUP * COLS
N_GROUP = N_DEV // GROUP
POS = 512
MSG = HD + LANES

F32 = jnp.float32
BF16 = jnp.bfloat16


def lane_of(shape):
    return lax.broadcasted_iota(jnp.int32, shape, len(shape) - 1)


def tiles_to_chunks(tiles):
    lane = lane_of(tiles[0].shape)
    t = tiles
    return (
        (t[0], t[1]),
        (jnp.where(lane < 96, t[2], t[1]), jnp.where(lane < 96, t[3], t[2])),
        (jnp.where(lane < 64, t[4], t[3]), jnp.where(lane < 64, t[5], t[4])),
        (jnp.where(lane < 32, t[6], t[5]), t[6]),
    )


def chunks_to_tiles(chunks):
    (a0, b0), (a1, b1), (a2, b2), (a3, b3) = chunks
    lane = lane_of(a0.shape)
    return (
        a0,
        jnp.where(lane < 96, b0, a1),
        jnp.where(lane < 96, a1, b1),
        jnp.where(lane < 64, b1, a2),
        jnp.where(lane < 64, a2, b2),
        jnp.where(lane < 32, b2, a3),
        jnp.where(lane < 32, a3, b3),
    )


def kernel(
    hidden_hbm, in_gain_hbm, w_latent_hbm, q_gain_hbm, w_query_hbm, keys_hbm, values_hbm, lengths_ref,
    w_out_hbm, post_gain_hbm, w_gate_hbm, w_up_hbm, w_down_hbm,
    out_ref,
    hidden_v, in_gain_v, q_gain_v, post_gain_v, w_latent, w_query, keys, values, w_out, w_gate, w_up, w_down,
    pad_hidden, pad_gain, s1, r1, s2, r2, s3, r3, q_wide, o_wide, s4, r4, s5, r5, s6, r6, x_all, s7, r7,
    local_sem, send_sem, recv_sem,
):
    p = lax.axis_index("pool")
    d = lax.axis_index("dev")

    barrier = pltpu.get_barrier_semaphore()

    def greet(k, carry):
        t = lax.rem(p * N_DEV + d + k, N_ALL)
        pl.semaphore_signal(
            barrier, inc=1, device_id=(lax.div(t, N_DEV), lax.rem(t, N_DEV)), device_id_type=MESH
        )
        return carry

    lax.fori_loop(1, N_ALL, greet, 0)

    def fetch(i, source, target):
        return pltpu.make_async_copy(source, target, local_sem.at[i])

    fetches = [
        fetch(i, source, target)
        for i, (source, target) in enumerate(
            [
                (hidden_hbm, hidden_v),
                (in_gain_hbm, in_gain_v),
                (w_latent_hbm, w_latent),
                (q_gain_hbm, q_gain_v),
                (w_query_hbm, w_query),
                (keys_hbm, keys),
                (values_hbm, values),
                (w_out_hbm, w_out),
                (post_gain_hbm, post_gain_v),
                (w_gate_hbm, w_gate),
                (w_up_hbm, w_up),
                (w_down_hbm, w_down),
            ]
        )
    ]
    for copy in fetches:
        copy.start()
    (f_hidden, f_in_gain, f_latent, f_q_gain, f_query, f_keys, f_values, f_out, f_post_gain, f_gate, f_up, f_down) = fetches

    def send(i, source, target, pool, dev):
        pltpu.make_async_remote_copy(
            src_ref=source,
            dst_ref=target,
            send_sem=send_sem.at[i],
            recv_sem=recv_sem.at[i],
            device_id=(pool, dev),
            device_id_type=MESH,
        ).start()

    def landed(sem, i, ref, count):
        block = ref.at[pl.ds(0, count)]
        pltpu.make_async_copy(block, block, sem.at[i]).wait()

    def to_group(i, source, target):
        def step(k, carry):
            send(i, source, target, p, lax.rem(d + k, N_DEV))
            return carry

        lax.fori_loop(1, N_DEV, step, 0)

    pad_hidden[...] = jnp.zeros_like(pad_hidden)
    pad_gain[...] = jnp.zeros_like(pad_gain)
    f_hidden.wait()
    f_in_gain.wait()
    hidden_f = hidden_v[...].astype(F32)
    pad_hidden[:, :COLS] = hidden_f
    square_part = jnp.sum(hidden_f * hidden_f, axis=1, keepdims=True)
    scaled_in = (hidden_f * in_gain_v[...]).astype(BF16)
    f_latent.wait()
    part = jnp.dot(scaled_in, w_latent[...], preferred_element_type=F32)
    for c in range(CHUNKS - 1):
        s1[c] = part[:, c * LANES : (c + 1) * LANES]
    s1[CHUNKS - 1] = jnp.broadcast_to(square_part, (ROWS, LANES))

    pl.semaphore_wait(barrier, N_ALL - 1)

    def send_latent(k, carry):
        c = lax.rem(d + k, CHUNKS)

        @pl.when(c != d)
        def _():
            send(0, s1.at[c], r1.at[d], p, c)

        return carry

    lax.fori_loop(0, CHUNKS, send_latent, 0)

    @pl.when(d < CHUNKS)
    def _():
        r1[d] = s1[d]
        landed(recv_sem, 0, r1, N_DEV - 1)
        total = jnp.sum(r1[...], axis=0)
        s2[...] = total
        r2[d] = total
        to_group(1, s2, r2.at[d])
        landed(recv_sem, 1, r2, CHUNKS - 1)

    @pl.when(d >= CHUNKS)
    def _():
        landed(recv_sem, 1, r2, CHUNKS)

    row_scale = lax.rsqrt(r2[CHUNKS - 1] * (1.0 / D) + EPS)
    latents = [r2[c] * row_scale for c in range(CHUNKS - 1)]
    squares = latents[0] * latents[0]
    for c in range(1, QR // LANES):
        squares = squares + latents[c] * latents[c]
    latent_mean = jnp.sum(squares, axis=1, keepdims=True) * (1.0 / QR)
    query_latent = jnp.concatenate(latents[: QR // LANES], axis=1)
    f_q_gain.wait()
    query_normed = (query_latent * lax.rsqrt(latent_mean + EPS) * q_gain_v[...]).astype(BF16)
    f_query.wait()
    query = jnp.dot(query_normed, w_query[...], preferred_element_type=F32)
    query_rows = jnp.concatenate([query[:, :HD], query[:, HD:]], axis=0).astype(BF16)
    s3[...] = query_rows
    r3[d] = query_rows
    to_group(2, s3, r3.at[d])

    def wide_new(first):
        new = jnp.concatenate(latents[first : first + HD // LANES], axis=1).astype(BF16).astype(F32)
        return jnp.concatenate([new, new], axis=0)

    key_new = wide_new(QR // LANES)
    value_new = wide_new((QR + HD) // LANES)
    scale_inv = 1.0 / math.sqrt(HD)
    score_new = jnp.sum(query_rows.astype(F32) * key_new, axis=1, keepdims=True) * scale_inv

    landed(recv_sem, 2, r3, N_DEV - 1)
    q_all = r3[...].reshape(N_DEV * 2 * ROWS, HD).astype(F32)
    q_wide[0] = q_all[:, :LANES]
    q_wide[1] = q_all[:, LANES:]
    f_keys.wait()
    f_values.wait()

    def attend(r, carry):
        own = pl.ds(r, H, stride=ROWS)
        q = jnp.concatenate([q_wide[0, own, :], q_wide[1, own, :]], axis=1).astype(BF16)
        scores = (
            lax.dot_general(q, keys[r], (((1,), (1,)), ((), ())), preferred_element_type=F32) * scale_inv
        )
        position = d * POS + lax.broadcasted_iota(jnp.int32, (H, POS), 1)
        valid = position < lengths_ref[r]
        masked = jnp.where(valid, scores, NEG)
        top = jnp.max(masked, axis=1, keepdims=True)
        weights = jnp.where(valid, jnp.exp(masked - top), 0.0)
        mass = jnp.sum(weights, axis=1, keepdims=True)
        summed = jnp.dot(weights.astype(BF16), values[r], preferred_element_type=F32)
        some = mass > 0.0
        safe = jnp.where(some, mass, 1.0)
        mean = summed / safe
        log_mass = jnp.where(some, top + jnp.log(safe), NEG)
        o_wide[0, own, :] = mean[:, :LANES]
        o_wide[1, own, :] = mean[:, LANES:]
        o_wide[2, own, :] = jnp.broadcast_to(log_mass, (H, LANES))
        return carry

    lax.fori_loop(0, ROWS, attend, 0)

    def pack(k, carry):
        j = lax.rem(d + k, N_DEV)
        rows = pl.ds(pl.multiple_of(j * 2 * ROWS, 2 * ROWS), 2 * ROWS)
        s4[j, :, :LANES] = o_wide[0, rows, :].astype(BF16)
        s4[j, :, LANES:HD] = o_wide[1, rows, :].astype(BF16)
        log_mass = o_wide[2, rows, :]
        high = log_mass.astype(BF16).astype(F32)
        rest = log_mass - high
        middle = rest.astype(BF16).astype(F32)
        low = rest - middle
        lane = lane_of(log_mass.shape)
        s4[j, :, HD:] = jnp.where(lane == 0, high, jnp.where(lane == 1, middle, low)).astype(BF16)

        @pl.when(k > 0)
        def _():
            send(3, s4.at[j], r4.at[d], p, j)

        return carry

    lax.fori_loop(0, N_DEV, pack, 0)
    r4[d] = s4[d]
    landed(recv_sem, 3, r4, N_DEV - 1)

    pieces = r4[:, :, HD:].astype(F32)
    log_all = jnp.sum(jnp.where(lane_of(pieces.shape) < 3, pieces, 0.0), axis=2, keepdims=True)
    top_all = jnp.maximum(jnp.max(log_all, axis=0), score_new)
    share = jnp.exp(log_all - top_all[None])
    fresh = jnp.exp(score_new - top_all)
    mass_all = jnp.sum(share, axis=0) + fresh
    numerator = jnp.sum(share * r4[:, :, :HD].astype(F32), axis=0)
    numerator = numerator + fresh.astype(BF16).astype(F32) * value_new
    attended = numerator / mass_all
    own_heads = jnp.concatenate([attended[:ROWS], attended[ROWS:]], axis=1).astype(BF16)

    f_out.wait()

    def project(i, carry):
        g = lax.rem(lax.div(d, GROUP) + i, N_GROUP)
        columns = pl.ds(pl.multiple_of(g * GROUP_COLS, LANES), GROUP_COLS)
        block = jnp.dot(own_heads, w_out[:, columns], preferred_element_type=F32)
        tiles = [block[:, t * LANES : (t + 1) * LANES] for t in range(GROUP_COLS // LANES)]
        for c, (low_half, high_half) in enumerate(tiles_to_chunks(tiles)):
            j = g * GROUP + c
            s5[j] = jnp.concatenate([low_half, high_half], axis=0).astype(BF16)

            @pl.when(j != d)
            def _():
                send(4, s5.at[j], r5.at[d], p, j)

        return carry

    lax.fori_loop(0, N_GROUP, project, 0)
    r5[d] = s5[d]

    turn = lax.rem(d * (COLS % LANES), LANES)
    back = lax.rem(LANES - turn, LANES)
    f_post_gain.wait()
    pad_gain[:, :COLS] = post_gain_v[...]
    lane = lane_of((ROWS, LANES))

    def unrotated(total):
        low_half = pltpu.roll(total[:ROWS], back, 1)
        high_half = pltpu.roll(total[ROWS:], back, 1)
        return low_half, jnp.where(lane < COLS - LANES, high_half, 0.0)

    landed(recv_sem, 4, r5, N_DEV - 1)
    attn_low, attn_high = unrotated(jnp.sum(r5[...].astype(F32), axis=0))
    res_low = pad_hidden[:, :LANES] + attn_low
    res_high = pad_hidden[:, LANES:] + attn_high
    row_squares = jnp.sum(res_low * res_low + res_high * res_high, axis=1, keepdims=True)
    coarse = row_squares.astype(BF16).astype(F32)
    fine = row_squares - coarse
    gained_low = res_low * pad_gain[:, :LANES]
    gained_high = res_high * pad_gain[:, LANES:]
    gained_high = jnp.where(lane == 96, coarse, jnp.where(lane == 97, fine, gained_high))
    tile = jnp.concatenate([pltpu.roll(gained_low, turn, 1), pltpu.roll(gained_high, turn, 1)], axis=0).astype(BF16)
    s6[...] = tile
    own = d * N_POOL + p
    r6[own] = tile

    def send_rows(k, carry):
        t = lax.rem(p * N_DEV + d + k, N_ALL)
        send(5, s6, r6.at[own], lax.div(t, N_DEV), lax.rem(t, N_DEV))
        return carry

    lax.fori_loop(1, N_ALL, send_rows, 0)
    landed(recv_sem, 5, r6, N_ALL - 1)

    all_rows = N_POOL * ROWS

    def assemble(g, sums):
        first = pl.multiple_of(g * GROUP * N_POOL, GROUP * N_POOL)
        block = r6[pl.ds(first, GROUP * N_POOL)].astype(F32).reshape(GROUP, N_POOL, 2, ROWS, LANES)
        chunks = [
            (block[c, :, 0].reshape(all_rows, LANES), block[c, :, 1].reshape(all_rows, LANES)) for c in range(GROUP)
        ]
        columns = pl.ds(pl.multiple_of(g * GROUP_COLS, LANES), GROUP_COLS)
        x_all[:, columns] = jnp.concatenate(chunks_to_tiles(chunks), axis=1).astype(BF16)
        return tuple(total + chunk[1] for total, chunk in zip(sums, chunks))

    zeros = jnp.zeros((all_rows, LANES), F32)
    sums = lax.fori_loop(0, N_GROUP, assemble, (zeros,) * GROUP)
    lane_all = lane_of((all_rows, LANES))
    kept = zeros
    for c in range(GROUP):
        at = (96 + c * (COLS % LANES)) % LANES
        kept = kept + jnp.where((lane_all == at) | (lane_all == at + 1), sums[c], 0.0)
    all_squares = jnp.sum(kept, axis=1, keepdims=True)
    norm = lax.rsqrt(all_squares * (1.0 / D) + EPS)

    f_gate.wait()
    f_up.wait()
    transposed = (((1,), (1,)), ((), ()))
    gate = lax.dot_general(x_all[...], w_gate[...], transposed, preferred_element_type=F32) * norm
    up = lax.dot_general(x_all[...], w_up[...], transposed, preferred_element_type=F32) * norm
    activated = (gate / (1.0 + jnp.exp(-gate)) * up).astype(BF16)

    f_down.wait()

    def give(i, carry):
        g = lax.rem(lax.div(d, GROUP) + i, N_GROUP)
        columns = pl.ds(pl.multiple_of(g * GROUP_COLS, LANES), GROUP_COLS)
        block = jnp.dot(activated, w_down[:, columns], preferred_element_type=F32)
        tiles = [block[:, t * LANES : (t + 1) * LANES] for t in range(GROUP_COLS // LANES)]
        for c, (low_half, high_half) in enumerate(tiles_to_chunks(tiles)):
            j = g * GROUP + c
            for q in range(N_POOL):
                rows = slice(q * ROWS, (q + 1) * ROWS)
                at = j * N_POOL + q
                s7[at] = jnp.concatenate([low_half[rows], high_half[rows]], axis=0).astype(BF16)

                @pl.when(at != own)
                def _():
                    send(6, s7.at[at], r7.at[own], q, j)

        return carry

    lax.fori_loop(0, N_GROUP, give, 0)
    r7[own] = s7[own]
    landed(recv_sem, 6, r7, N_ALL - 1)
    ffn_low, ffn_high = unrotated(jnp.sum(r7[...].astype(F32), axis=0))
    out_ref[:, :LANES] = res_low + ffn_low
    out_ref[:, LANES:] = (res_high + ffn_high)[:, : COLS - LANES]

    @pl.when(d < CHUNKS)
    def _():
        landed(send_sem, 0, s1, CHUNKS - 1)
        landed(send_sem, 1, r1, N_DEV - 1)

    @pl.when(d >= CHUNKS)
    def _():
        landed(send_sem, 0, s1, CHUNKS)

    landed(send_sem, 2, r3, N_DEV - 1)
    landed(send_sem, 3, r4, N_DEV - 1)
    landed(send_sem, 4, r5, N_DEV - 1)
    landed(send_sem, 5, r6, N_ALL - 1)
    landed(send_sem, 6, r7, N_ALL - 1)


def local(
    hidden_in, in_gain, w_latent, q_gain, w_query, cache_keys, cache_values, lengths, w_out, post_gain,
    w_gate, w_up, w_down,
):
    operands = (
        hidden_in, in_gain[None, :], w_latent, q_gain[None, :], w_query, cache_keys, cache_values, lengths,
        w_out, post_gain[None, :], w_gate.T, w_up.T, w_down,
    )
    specs = [pl.BlockSpec(memory_space=pl.ANY)] * len(operands)
    specs[7] = pl.BlockSpec(memory_space=pltpu.SMEM)
    tile = (2 * ROWS, LANES)

    def like(array):
        return pltpu.VMEM(array.shape, array.dtype)

    scratch = [
        like(hidden_in),
        pltpu.VMEM((1, COLS), F32),
        pltpu.VMEM((1, QR), F32),
        pltpu.VMEM((1, COLS), F32),
        like(w_latent),
        like(w_query),
        like(cache_keys),
        like(cache_values),
        like(w_out),
        pltpu.VMEM(w_gate.shape[::-1], BF16),
        pltpu.VMEM(w_up.shape[::-1], BF16),
        like(w_down),
        pltpu.VMEM((ROWS, 2 * LANES), F32),
        pltpu.VMEM((1, 2 * LANES), F32),
        pltpu.VMEM((CHUNKS, ROWS, LANES), F32),
        pltpu.VMEM((N_DEV, ROWS, LANES), F32),
        pltpu.VMEM((ROWS, LANES), F32),
        pltpu.VMEM((CHUNKS, ROWS, LANES), F32),
        pltpu.VMEM((2 * ROWS, HD), BF16),
        pltpu.VMEM((N_DEV, 2 * ROWS, HD), BF16),
        pltpu.VMEM((HD // LANES, H * ROWS, LANES), F32),
        pltpu.VMEM((MSG // LANES, H * ROWS, LANES), F32),
        pltpu.VMEM((N_DEV, 2 * ROWS, MSG), BF16),
        pltpu.VMEM((N_DEV, 2 * ROWS, MSG), BF16),
        pltpu.VMEM((N_DEV, *tile), BF16),
        pltpu.VMEM((N_DEV, *tile), BF16),
        pltpu.VMEM(tile, BF16),
        pltpu.VMEM((N_ALL, *tile), BF16),
        pltpu.VMEM((N_POOL * ROWS, D), BF16),
        pltpu.VMEM((N_ALL, *tile), BF16),
        pltpu.VMEM((N_ALL, *tile), BF16),
        pltpu.SemaphoreType.DMA((12,)),
        pltpu.SemaphoreType.DMA((7,)),
        pltpu.SemaphoreType.DMA((7,)),
    ]
    return pl.pallas_call(
        kernel,
        out_shape=jax.ShapeDtypeStruct(hidden_in.shape, F32),
        in_specs=specs,
        out_specs=pl.BlockSpec(memory_space=pltpu.VMEM),
        scratch_shapes=scratch,
        compiler_params=pltpu.CompilerParams(
            collective_id=0, has_side_effects=True, vmem_limit_bytes=56 * 2**20
        ),
    )(*operands)


def solution(mesh):
    placed = (
        P("pool", "dev"),
        P("dev"),
        P("dev", None),
        P(),
        P(None, "dev"),
        P("pool", "dev", None),
        P("pool", "dev", None),
        P("pool"),
        P("dev", None),
        P("dev"),
        P(None, ("pool", "dev")),
        P(None, ("pool", "dev")),
        P(("pool", "dev"), None),
    )
    return jax.shard_map(
        local, mesh=mesh, in_specs=placed, out_specs=P("pool", "dev"), check_vma=False
    )
```

time: 1950 us -> 73.6 us (0.04)
  waiting for transfers between devices: 1040 us -> 0 us
  blocking collectives: 787 us -> 0 us
  Pallas kernels: 0 us -> 71.1 us
  other arithmetic: 45.4 us -> 0 us
  local copies, waits for them, and re-layouts: 28.6 us -> 1.3 us
  matrix products: 27.2 us -> 0 us
    reduce_scatter x1 -> x0, waiting for transfers between devices: 647 us -> none  [local(): lax.psum_scatter(ffn_term, ('pool', 'dev'), scatter_dimension=0, tiled=True)]
    all_gather x4 -> x0, blocking collectives: 600 us -> none  [the longest x1 325 us: local(): lax.all_gather(normed, ('pool', 'dev'), axis=0, tiled=True)]
    psum x1 -> x0, waiting for transfers between devices: 222 us -> none  [local(): latent, squares = lax.psum((latent_part, square_part), 'dev')]
    psum x2 -> x0, blocking collectives: 187 us -> none  [the longest x1 97.4 us: local(): latent, squares = lax.psum((latent_part, square_part), 'dev')]
    unnamed x5 -> x0, waiting for transfers between devices: 174 us -> none
    pallas_call x0 -> x1, Pallas kernels: none -> 71.1 us  [local(): pl.pallas_call(kernel, out_shape=jax.ShapeDtypeStruct(hidden_in.shape, F3...]
    add x64 -> x0, other arithmetic: 41.8 us -> none  [the longest x31 40 us: combine_parts(): left_part[2] * left_factor[..., None]]
  transfers between devices with their start and end apart: 4 -> 0, of which waited for: 3 -> 0; matrix products, arithmetic and copies ran while one was open for 1% -> 0% of each run, Pallas kernels for 0% -> 0%
where the time goes in v1:
time: 73.6 us; the launch traced here: 72.4 us
  Pallas kernels  71.1 us (97%)
  local copies, waits for them, and re-layouts  1.3 us (2%)
    pallas_call x1, Pallas kernels, local(): pl.pallas_call(kernel, out_shape=jax.ShapeDtypeStruct(hidden_in.shape, F3...  71.1 us

profile of v1, /device:TPU:0, one launch (start us, length us, event | category | flops | bytes accessed | tf_op | source)
XLA Modules:
  0.0 72.4 jit_solution(17800993412129994165)
XLA Ops:
  0.0 71.1 %shard_map.127 = f32[8,224]{1,0:T(8,128)} custom-call(bf16[8,224]{1,0:T(8,128)(2,1)} %hidden_hbm.1, f32[1,224]{1,0:T(1,128)} %bitcast.8, bf16[224,2560]{1,0:T(8,128)(2,1)} %w_latent_hbm.1, f32[1,2048]{1,0:T(1,128)} %bitcast.7, bf16[2048,512]{1,0:T(8,128)(2,1)} %w_query_hbm.1, bf16[8,512,256]{2,1,0:T(8,128)(2,1)} %keys_hbm.1, ...), custom_call_target="tpu_custom_call" | custom-call | tf_op jit(solution)/shard_map/pallas_call | solution.py:441
  71.1 1.3 %copy.15 = f32[8,224]{1,0:T(8,128)} copy(f32[8,224]{1,0:T(8,128)} %shard_map.127) | data formatting | bytes 14336

commit v2 on v1

v2 whole, which is shorter than its diff:
```python
import math

import jax
import jax.numpy as jnp
from jax import lax
from jax.experimental import pallas as pl
from jax.experimental.pallas import tpu as pltpu
from jax.sharding import PartitionSpec as P

D = 7168
H = 64
HD = 256
QR = 2048
EPS = 1e-05
NEG = -1e30
MESH = pl.DeviceIdType.MESH

N_POOL = 4
N_DEV = 32
N_HALF = 2 * N_DEV
ROWS = 8
COLS = 224
LANES = 128
CHUNKS = (QR + 2 * HD) // LANES + 1
GROUP = 4
GROUP_COLS = GROUP * COLS
N_GROUP = N_DEV // GROUP
POS = 512
MSG = HD + LANES
UNROLL = 8

F32 = jnp.float32
BF16 = jnp.bfloat16


def lane_of(shape):
    return lax.broadcasted_iota(jnp.int32, shape, len(shape) - 1)


def tiles_to_chunks(tiles):
    lane = lane_of(tiles[0].shape)
    t = tiles
    return (
        (t[0], t[1]),
        (jnp.where(lane < 96, t[2], t[1]), jnp.where(lane < 96, t[3], t[2])),
        (jnp.where(lane < 64, t[4], t[3]), jnp.where(lane < 64, t[5], t[4])),
        (jnp.where(lane < 32, t[6], t[5]), t[6]),
    )


def chunks_to_tiles(chunks):
    (a0, b0), (a1, b1), (a2, b2), (a3, b3) = chunks
    lane = lane_of(a0.shape)
    return (
        a0,
        jnp.where(lane < 96, b0, a1),
        jnp.where(lane < 96, a1, b1),
        jnp.where(lane < 64, b1, a2),
        jnp.where(lane < 64, a2, b2),
        jnp.where(lane < 32, b2, a3),
        jnp.where(lane < 32, a3, b3),
    )


def packed(values, bits):
    word = sum(value << (bits * k) for k, value in enumerate(values))
    return word - 2**32 if word >= 2**31 else word


FAR = ((2, 2), (2, 1), (1, 2), (2, 3), (3, 2), (1, 1), (3, 3), (1, 3), (3, 1), (2, 0), (0, 2), (1, 0), (0, 1), (3, 0), (0, 3), (0, 0))
FAR_X = packed([step[0] for step in FAR], 2)
FAR_Y = packed([step[1] for step in FAR], 2)
FAR_GROUP_X = packed([2, 2, 1, 3, 1, 3, 0, 0], 2)
FAR_GROUP_Y = packed([1, 0, 1, 1, 0, 0, 1, 0], 2)
PLANE = 16
EXTRA = CHUNKS - PLANE


def entry(word, k):
    return lax.bitwise_and(lax.shift_right_logical(jnp.int32(word), 2 * k), 3)


def kernel(
    hidden_hbm, in_gain_hbm, w_latent_hbm, q_gain_hbm, w_query_hbm, keys_hbm, values_hbm, lengths_hbm,
    w_out_hbm, post_gain_hbm, w_gate_hbm, w_up_hbm, w_down_hbm,
    out_ref,
    hidden_v, in_gain_v, q_gain_v, post_gain_v, lengths, w_latent, w_query, keys, values, w_out, w_gate, w_up, w_down,
    pad_hidden, pad_gain, s1, r1, s2, r2, s3, r3, q_wide, o_wide, s4, r4, s5, r5, s6, r6, x_all, kept, t7, u7, s7, r7,
    local_sem, send_sem, recv_sem, pair_sem,
):
    p = lax.axis_index("pool")
    d = lax.axis_index("dev")
    x = lax.div(d, 8)
    y = lax.rem(lax.div(d, 2), 4)
    z_high = lax.rem(d, 2)
    z_low = lax.div(p, 2)
    core = lax.rem(p, 2)
    plane = lax.div(d, 2)
    sibling = z_low * 2 + 1 - core

    def peer(i, dz):
        there = lax.rem(x + entry(FAR_X, i), 4) * 8 + lax.rem(y + entry(FAR_Y, i), 4) * 2
        return there + lax.rem(z_high + dz, 2)

    def peer_all(n):
        part = lax.rem(n, 4)
        there = peer(lax.div(n, 4), 1 - lax.div(part, 2))
        return lax.rem(z_low + lax.rem(lax.div(part + 1, 2), 2), 2) * 2 + core, there

    def fetch(i, source, target):
        copy = pltpu.make_async_copy(source, target, local_sem.at[i])
        copy.start()
        return copy

    f_hidden = fetch(0, hidden_hbm, hidden_v)
    f_in_gain = fetch(1, in_gain_hbm, in_gain_v)
    f_latent = fetch(2, w_latent_hbm, w_latent)

    barrier = pltpu.get_barrier_semaphore()

    def greet(n, carry):
        pl.semaphore_signal(barrier, inc=1, device_id=peer_all(n), device_id_type=MESH)
        return carry

    lax.fori_loop(0, N_HALF - 1, greet, 0)
    pl.semaphore_signal(barrier, inc=1, device_id=(sibling, d), device_id_type=MESH)

    f_q_gain = fetch(3, q_gain_hbm, q_gain_v)
    f_query = fetch(4, w_query_hbm, w_query)
    f_keys = fetch(5, keys_hbm, keys)
    f_lengths = fetch(6, lengths_hbm, lengths)
    f_values = fetch(7, values_hbm, values)
    f_out = fetch(8, w_out_hbm, w_out)
    f_post_gain = fetch(9, post_gain_hbm, post_gain_v)
    f_gate = fetch(10, w_gate_hbm, w_gate)
    f_up = fetch(11, w_up_hbm, w_up)
    f_down = fetch(12, w_down_hbm, w_down)

    def remote(i, source, target, pool, dev):
        return pltpu.make_async_remote_copy(
            src_ref=source,
            dst_ref=target,
            send_sem=send_sem.at[i],
            recv_sem=recv_sem.at[i],
            device_id=(pool, dev),
            device_id_type=MESH,
        )

    def send(*args):
        remote(*args).start()

    def landed(sem, i, ref, count):
        block = ref.at[pl.ds(0, count)]
        pltpu.make_async_copy(block, block, sem.at[i]).wait()

    def to_group(i, source, target):
        def step(n, carry):
            send(i, source, target, p, peer(lax.rem(n, 16), 1 - lax.div(n, 16)))
            return carry

        lax.fori_loop(0, N_DEV - 1, step, 0)

    pad_hidden[...] = jnp.zeros_like(pad_hidden)
    pad_gain[...] = jnp.zeros_like(pad_gain)
    f_hidden.wait()
    f_in_gain.wait()
    hidden_f = hidden_v[...].astype(F32)
    pad_hidden[:, :COLS] = hidden_f
    square_part = jnp.sum(hidden_f * hidden_f, axis=1, keepdims=True)
    scaled_in = (hidden_f * in_gain_v[...]).astype(BF16)
    f_latent.wait()
    part = jnp.dot(scaled_in, w_latent[...], preferred_element_type=F32)
    for c in range(CHUNKS - 1):
        s1[2 * (c % PLANE) + c // PLANE] = part[:, c * LANES : (c + 1) * LANES]
    s1[2 * (EXTRA - 1) + 1] = jnp.broadcast_to(square_part, (ROWS, LANES))

    pl.semaphore_wait(barrier, N_HALF)

    def send_latent(n, carry):
        j = peer(n, 0)
        owner = lax.div(j, 2)

        @pl.when(owner < EXTRA)
        def _():
            send(0, s1.at[pl.ds(2 * owner, 2)], r1.at[pl.ds(2 * plane, 2)], p, j)

        @pl.when(owner >= EXTRA)
        def _():
            send(0, s1.at[pl.ds(2 * owner, 1)], r1.at[pl.ds(2 * plane, 1)], p, j)

        return carry

    lax.fori_loop(0, PLANE - 1, send_latent, 0)

    def spread(tiles):
        r1[pl.ds(2 * plane, tiles)] = s1[pl.ds(2 * plane, tiles)]
        landed(recv_sem, 0, r1, (PLANE - 1) * tiles)
        for t in range(tiles):
            total = r1[t]
            for source in range(1, PLANE):
                total = total + r1[2 * source + t]
            s2[t] = total
            r2[2 * d + t] = total
        to_group(1, s2.at[pl.ds(0, tiles)], r2.at[pl.ds(2 * d, tiles)])
        landed(recv_sem, 1, r2, 2 * CHUNKS - tiles)

    @pl.when(plane < EXTRA)
    def _():
        spread(2)

    @pl.when(plane >= EXTRA)
    def _():
        spread(1)

    def summed_chunk(c):
        at = 4 * (c % PLANE) + c // PLANE
        return r2[at] + r2[at + 2]

    row_scale = lax.rsqrt(summed_chunk(CHUNKS - 1) * (1.0 / D) + EPS)
    latents = [summed_chunk(c) * row_scale for c in range(CHUNKS - 1)]
    squares = latents[0] * latents[0]
    for c in range(1, QR // LANES):
        squares = squares + latents[c] * latents[c]
    latent_mean = jnp.sum(squares, axis=1, keepdims=True) * (1.0 / QR)
    query_latent = jnp.concatenate(latents[: QR // LANES], axis=1)
    f_q_gain.wait()
    query_normed = (query_latent * lax.rsqrt(latent_mean + EPS) * q_gain_v[...]).astype(BF16)
    f_query.wait()
    query = jnp.dot(query_normed, w_query[...], preferred_element_type=F32)
    query_rows = jnp.concatenate([query[:, :HD], query[:, HD:]], axis=0).astype(BF16)
    s3[...] = query_rows
    r3[d] = query_rows
    to_group(2, s3, r3.at[d])

    def wide_new(first):
        new = jnp.concatenate(latents[first : first + HD // LANES], axis=1).astype(BF16).astype(F32)
        return jnp.concatenate([new, new], axis=0)

    key_new = wide_new(QR // LANES)
    value_new = wide_new((QR + HD) // LANES)
    scale_inv = 1.0 / math.sqrt(HD)
    score_new = jnp.sum(query_rows.astype(F32) * key_new, axis=1, keepdims=True) * scale_inv

    f_keys.wait()
    f_lengths.wait()
    f_values.wait()
    landed(recv_sem, 2, r3, N_DEV - 1)
    q_all = r3[...].reshape(N_DEV * 2 * ROWS, HD).astype(F32)
    q_wide[0] = q_all[:, :LANES]
    q_wide[1] = q_all[:, LANES:]

    def attend(r, carry):
        own = pl.ds(r, H, stride=ROWS)
        q = jnp.concatenate([q_wide[0, own, :], q_wide[1, own, :]], axis=1).astype(BF16)
        scores = (
            lax.dot_general(q, keys[r], (((1,), (1,)), ((), ())), preferred_element_type=F32) * scale_inv
        )
        position = d * POS + lax.broadcasted_iota(jnp.int32, (H, POS), 1)
        valid = position < lengths[r]
        masked = jnp.where(valid, scores, NEG)
        top = jnp.max(masked, axis=1, keepdims=True)
        weights = jnp.where(valid, jnp.exp(masked - top), 0.0)
        mass = jnp.sum(weights, axis=1, keepdims=True)
        summed = jnp.dot(weights.astype(BF16), values[r], preferred_element_type=F32)
        some = mass > 0.0
        safe = jnp.where(some, mass, 1.0)
        mean = summed / safe
        log_mass = jnp.where(some, top + jnp.log(safe), NEG)
        o_wide[0, own, :] = mean[:, :LANES]
        o_wide[1, own, :] = mean[:, LANES:]
        o_wide[2, own, :] = jnp.broadcast_to(log_mass, (H, LANES))
        return carry

    lax.fori_loop(0, ROWS, attend, 0, unroll=UNROLL)

    def pack(n, carry):
        j = peer(lax.rem(n, 16), 1 - lax.div(n, 16))
        rows = pl.ds(pl.multiple_of(j * 2 * ROWS, 2 * ROWS), 2 * ROWS)
        s4[j, :, :LANES] = o_wide[0, rows, :].astype(BF16)
        s4[j, :, LANES:HD] = o_wide[1, rows, :].astype(BF16)
        log_mass = o_wide[2, rows, :]
        high = log_mass.astype(BF16).astype(F32)
        rest = log_mass - high
        middle = rest.astype(BF16).astype(F32)
        low = rest - middle
        lane = lane_of(log_mass.shape)
        s4[j, :, HD:] = jnp.where(lane == 0, high, jnp.where(lane == 1, middle, low)).astype(BF16)

        @pl.when(n < N_DEV - 1)
        def _():
            send(3, s4.at[j], r4.at[d], p, j)

        return carry

    lax.fori_loop(0, N_DEV, pack, 0)
    r4[d] = s4[d]
    landed(recv_sem, 3, r4, N_DEV - 1)

    pieces = r4[:, :, HD:].astype(F32)
    log_all = jnp.sum(jnp.where(lane_of(pieces.shape) < 3, pieces, 0.0), axis=2, keepdims=True)
    top_all = jnp.maximum(jnp.max(log_all, axis=0), score_new)
    share = jnp.exp(log_all - top_all[None])
    fresh = jnp.exp(score_new - top_all)
    mass_all = jnp.sum(share, axis=0) + fresh
    numerator = jnp.sum(share * r4[:, :, :HD].astype(F32), axis=0)
    numerator = numerator + fresh.astype(BF16).astype(F32) * value_new
    attended = numerator / mass_all
    own_heads = jnp.concatenate([attended[:ROWS], attended[ROWS:]], axis=1).astype(BF16)

    f_out.wait()

    def group_at(i):
        return lax.rem(x + entry(FAR_GROUP_X, i), 4) * 2 + lax.rem(lax.div(y, 2) + entry(FAR_GROUP_Y, i), 2)

    def columns_of(g):
        return pl.ds(pl.multiple_of(g * GROUP_COLS, LANES), GROUP_COLS)

    def chunks_of(block):
        return tiles_to_chunks([block[:, t * LANES : (t + 1) * LANES] for t in range(GROUP_COLS // LANES)])

    def project(i, carry):
        g = group_at(i)
        block = jnp.dot(own_heads, w_out[:, columns_of(g)], preferred_element_type=F32)
        for c, halves in enumerate(chunks_of(block)):
            j = g * GROUP + c
            s5[j] = jnp.concatenate(halves, axis=0).astype(BF16)

            @pl.when(j != d)
            def _():
                send(4, s5.at[j], r5.at[d], p, j)

        return carry

    lax.fori_loop(0, N_GROUP, project, 0)
    r5[d] = s5[d]

    turn = lax.rem(d * (COLS % LANES), LANES)
    back = lax.rem(LANES - turn, LANES)
    f_post_gain.wait()
    pad_gain[:, :COLS] = post_gain_v[...]
    lane = lane_of((ROWS, LANES))

    def unrotated(total):
        low_half = pltpu.roll(total[:ROWS], back, 1)
        high_half = pltpu.roll(total[ROWS:], back, 1)
        return low_half, jnp.where(lane < COLS - LANES, high_half, 0.0)

    landed(recv_sem, 4, r5, N_DEV - 1)
    attn_low, attn_high = unrotated(jnp.sum(r5[...].astype(F32), axis=0))
    res_low = pad_hidden[:, :LANES] + attn_low
    res_high = pad_hidden[:, LANES:] + attn_high
    row_squares = jnp.sum(res_low * res_low + res_high * res_high, axis=1, keepdims=True)
    coarse = row_squares.astype(BF16).astype(F32)
    fine = row_squares - coarse
    gained_low = res_low * pad_gain[:, :LANES]
    gained_high = res_high * pad_gain[:, LANES:]
    gained_high = jnp.where(lane == 96, coarse, jnp.where(lane == 97, fine, gained_high))
    tile = jnp.concatenate([pltpu.roll(gained_low, turn, 1), pltpu.roll(gained_high, turn, 1)], axis=0).astype(BF16)
    s6[...] = tile
    own = d * 2 + z_low
    r6[core, own] = tile

    def send_rows(n, carry):
        send(5, s6, r6.at[core, own], *peer_all(n))
        return carry

    lax.fori_loop(0, N_HALF - 1, send_rows, 0)
    landed(recv_sem, 5, r6.at[0], N_HALF - 1)
    forward = remote(6, r6.at[core], r6.at[core], sibling, d)
    forward.start()
    forward.wait_recv()

    all_rows = N_POOL * ROWS

    def assemble(g, sums):
        first = pl.multiple_of(g * 2 * GROUP, 2 * GROUP)
        block = r6[:, pl.ds(first, 2 * GROUP)].astype(F32).reshape(2, GROUP, 2, 2, ROWS, LANES)
        chunks = [
            (block[:, c, :, 0].reshape(all_rows, LANES), block[:, c, :, 1].reshape(all_rows, LANES))
            for c in range(GROUP)
        ]
        x_all[:, columns_of(g)] = jnp.concatenate(chunks_to_tiles(chunks), axis=1).astype(BF16)
        return tuple(total + chunk[1] for total, chunk in zip(sums, chunks))

    zeros = jnp.zeros((all_rows, LANES), F32)
    sums = lax.fori_loop(0, N_GROUP, assemble, (zeros,) * GROUP)
    lane_all = lane_of((all_rows, LANES))
    squares_at = zeros
    for c in range(GROUP):
        at = (96 + c * (COLS % LANES)) % LANES
        squares_at = squares_at + jnp.where((lane_all == at) | (lane_all == at + 1), sums[c], 0.0)
    all_squares = jnp.sum(squares_at, axis=1, keepdims=True)
    norm = lax.rsqrt(all_squares * (1.0 / D) + EPS)

    f_gate.wait()
    f_up.wait()
    transposed = (((1,), (1,)), ((), ()))
    gate = lax.dot_general(x_all[...], w_gate[...], transposed, preferred_element_type=F32) * norm
    up = lax.dot_general(x_all[...], w_up[...], transposed, preferred_element_type=F32) * norm
    activated = (gate / (1.0 + jnp.exp(-gate)) * up).astype(BF16)

    f_down.wait()

    def give(i, carry):
        g = group_at(i)
        block = jnp.dot(activated, w_down[:, columns_of(g)], preferred_element_type=F32)
        for c, (low_half, high_half) in enumerate(chunks_of(block)):
            for q in range(N_POOL):
                rows = slice(q * ROWS, (q + 1) * ROWS)
                whole = jnp.concatenate([low_half[rows], high_half[rows]], axis=0)

                @pl.when(core == q // 2)
                def _():
                    kept[g, 2 * c + q % 2] = whole

                @pl.when(core != q // 2)
                def _():
                    t7[g, 2 * c + q % 2] = whole.astype(BF16)

        pltpu.make_async_remote_copy(
            src_ref=t7.at[g],
            dst_ref=u7.at[g],
            send_sem=send_sem.at[7],
            recv_sem=pair_sem.at[g],
            device_id=(sibling, d),
            device_id_type=MESH,
        ).start()
        return carry

    lax.fori_loop(0, N_GROUP, give, 0)

    def pass_on(i, carry):
        g = group_at(i)
        pltpu.make_async_copy(u7.at[g], u7.at[g], pair_sem.at[g]).wait()
        first = pl.multiple_of(g * 2 * GROUP, 2 * GROUP)
        s7[pl.ds(first, 2 * GROUP)] = (kept[g] + u7[g].astype(F32)).astype(BF16)
        for c in range(GROUP):
            for q in range(2):
                at = first + 2 * c + q

                @pl.when(at != own)
                def _():
                    send(8, s7.at[at], r7.at[own], q * 2 + core, g * GROUP + c)

        return carry

    lax.fori_loop(0, N_GROUP, pass_on, 0)
    r7[own] = s7[own]
    landed(recv_sem, 8, r7, N_HALF - 1)
    ffn_low, ffn_high = unrotated(jnp.sum(r7[...].astype(F32), axis=0))
    out_ref[:, :LANES] = res_low + ffn_low
    out_ref[:, LANES:] = (res_high + ffn_high)[:, : COLS - LANES]

    @pl.when(plane < EXTRA)
    def _():
        landed(send_sem, 0, s1, PLANE - 1 + EXTRA - 1)
        landed(send_sem, 1, r2, 2 * (N_DEV - 1))

    @pl.when(plane >= EXTRA)
    def _():
        landed(send_sem, 0, s1, PLANE - 1 + EXTRA)
        landed(send_sem, 1, r2, N_DEV - 1)

    landed(send_sem, 2, r3, N_DEV - 1)
    landed(send_sem, 3, r4, N_DEV - 1)
    landed(send_sem, 4, r5, N_DEV - 1)
    landed(send_sem, 5, r6.at[0], N_HALF - 1)
    forward.wait_send()
    landed(send_sem, 7, t7, N_GROUP)
    landed(send_sem, 8, r7, N_HALF - 1)


def local(
    hidden_in, in_gain, w_latent, q_gain, w_query, cache_keys, cache_values, lengths, w_out, post_gain,
    w_gate, w_up, w_down,
):
    operands = (
        hidden_in, in_gain[None, :], w_latent, q_gain[None, :], w_query, cache_keys, cache_values, lengths,
        w_out, post_gain[None, :], w_gate.T, w_up.T, w_down,
    )
    tile = (2 * ROWS, LANES)

    def like(array):
        return pltpu.VMEM(array.shape, array.dtype)

    scratch = [
        like(hidden_in),
        pltpu.VMEM((1, COLS), F32),
        pltpu.VMEM((1, QR), F32),
        pltpu.VMEM((1, COLS), F32),
        pltpu.SMEM(lengths.shape, jnp.int32),
        like(w_latent),
        like(w_query),
        like(cache_keys),
        like(cache_values),
        like(w_out),
        pltpu.VMEM(w_gate.shape[::-1], BF16),
        pltpu.VMEM(w_up.shape[::-1], BF16),
        like(w_down),
        pltpu.VMEM((ROWS, 2 * LANES), F32),
        pltpu.VMEM((1, 2 * LANES), F32),
        pltpu.VMEM((2 * PLANE, ROWS, LANES), F32),
        pltpu.VMEM((2 * PLANE, ROWS, LANES), F32),
        pltpu.VMEM((2, ROWS, LANES), F32),
        pltpu.VMEM((2 * N_DEV, ROWS, LANES), F32),
        pltpu.VMEM((2 * ROWS, HD), BF16),
        pltpu.VMEM((N_DEV, 2 * ROWS, HD), BF16),
        pltpu.VMEM((HD // LANES, H * ROWS, LANES), F32),
        pltpu.VMEM((MSG // LANES, H * ROWS, LANES), F32),
        pltpu.VMEM((N_DEV, 2 * ROWS, MSG), BF16),
        pltpu.VMEM((N_DEV, 2 * ROWS, MSG), BF16),
        pltpu.VMEM((N_DEV, *tile), BF16),
        pltpu.VMEM((N_DEV, *tile), BF16),
        pltpu.VMEM(tile, BF16),
        pltpu.VMEM((2, N_HALF, *tile), BF16),
        pltpu.VMEM((N_POOL * ROWS, D), BF16),
        pltpu.VMEM((N_GROUP, 2 * GROUP, *tile), F32),
        pltpu.VMEM((N_GROUP, 2 * GROUP, *tile), BF16),
        pltpu.VMEM((N_GROUP, 2 * GROUP, *tile), BF16),
        pltpu.VMEM((N_HALF, *tile), BF16),
        pltpu.VMEM((N_HALF, *tile), BF16),
        pltpu.SemaphoreType.DMA((13,)),
        pltpu.SemaphoreType.DMA((9,)),
        pltpu.SemaphoreType.DMA((9,)),
        pltpu.SemaphoreType.DMA((N_GROUP,)),
    ]
    return pl.pallas_call(
        kernel,
        out_shape=pltpu.VMEM(hidden_in.shape, F32),
        in_specs=[pl.BlockSpec(memory_space=pl.ANY)] * len(operands),
        out_specs=pl.BlockSpec(memory_space=pltpu.VMEM),
        scratch_shapes=scratch,
        compiler_params=pltpu.CompilerParams(
            collective_id=0, has_side_effects=True, vmem_limit_bytes=56 * 2**20
        ),
    )(*operands)


def solution(mesh):
    placed = (
        P("pool", "dev"),
        P("dev"),
        P("dev", None),
        P(),
        P(None, "dev"),
        P("pool", "dev", None),
        P("pool", "dev", None),
        P("pool"),
        P("dev", None),
        P("dev"),
        P(None, ("pool", "dev")),
        P(None, ("pool", "dev")),
        P(("pool", "dev"), None),
    )
    return jax.shard_map(
        local, mesh=mesh, in_specs=placed, out_specs=P("pool", "dev"), check_vma=False
    )
```

time: 73.6 us -> 62.7 us (0.85); the launches traced: 72.4 us -> 62.2 us
  Pallas kernels: 71.1 us -> 61.6 us
    pallas_call x1, Pallas kernels: 71.1 us -> 61.6 us  [local(): pl.pallas_call(kernel, out_shape=pltpu.VMEM(hidden_in.shape, F32), in_spe...]
where the time goes in v2:
time: 62.7 us; the launch traced here: 62.2 us
  Pallas kernels  61.6 us (98%)
    pallas_call x1, Pallas kernels, local(): pl.pallas_call(kernel, out_shape=pltpu.VMEM(hidden_in.shape, F32), in_spe...  61.6 us

profile of v2, /device:TPU:0, one launch (start us, length us, event | category | flops | bytes accessed | tf_op | source)
XLA Modules:
  0.0 62.2 jit_solution(5804379620078491615)
XLA Ops:
  0.0 61.6 %shard_map.127 = f32[8,224]{1,0:T(8,128)S(1)} custom-call(bf16[8,224]{1,0:T(8,128)(2,1)} %hidden_hbm.1, f32[1,224]{1,0:T(1,128)} %bitcast.8, bf16[224,2560]{1,0:T(8,128)(2,1)} %w_latent_hbm.1, f32[1,2048]{1,0:T(1,128)} %bitcast.7, bf16[2048,512]{1,0:T(8,128)(2,1)} %w_query_hbm.1, bf16[8,512,256]{2,1,0:T(8,128)(2,1)} %keys_hbm.1, ...), custom_call_target="tpu_custom_call" | custom-call | tf_op jit(solution)/shard_map/pallas_call | solution.py:527
  61.6 0.6 copy.15

commit v3 on v2

--- a/solution.py
+++ b/solution.py
@@ -85,8 +85,8 @@
     w_out_hbm, post_gain_hbm, w_gate_hbm, w_up_hbm, w_down_hbm,
     out_ref,
     hidden_v, in_gain_v, q_gain_v, post_gain_v, lengths, w_latent, w_query, keys, values, w_out, w_gate, w_up, w_down,
-    pad_hidden, pad_gain, s1, r1, s2, r2, s3, r3, q_wide, o_wide, s4, r4, s5, r5, s6, r6, x_all, kept, t7, u7, s7, r7,
-    local_sem, send_sem, recv_sem, pair_sem,
+    pad_hidden, pad_gain, s1, r1, s2, r2, s3, r3, q_wide, o_wide, s4, r4, s5, r5, s6, r6, x_all, s7, r7, keys_t,
+    local_sem, send_sem, recv_sem,
 ):
     p = lax.axis_index("pool")
     d = lax.axis_index("dev")
@@ -132,9 +132,9 @@
     f_values = fetch(7, values_hbm, values)
     f_out = fetch(8, w_out_hbm, w_out)
     f_post_gain = fetch(9, post_gain_hbm, post_gain_v)
-    f_gate = fetch(10, w_gate_hbm, w_gate)
-    f_up = fetch(11, w_up_hbm, w_up)
-    f_down = fetch(12, w_down_hbm, w_down)
+    f_gate = fetch(10, w_gate_hbm, w_gate.at[0])
+    f_up = fetch(11, w_up_hbm, w_up.at[0])
+    f_down = fetch(12, w_down_hbm, w_down.at[0])
 
     def remote(i, source, target, pool, dev):
         return pltpu.make_async_remote_copy(
@@ -191,6 +191,21 @@
         return carry
 
     lax.fori_loop(0, PLANE - 1, send_latent, 0)
+
+    shared = [
+        remote(6 + k, source, target.at[1], sibling, d)
+        for k, (source, target) in enumerate(((w_gate_hbm, w_gate), (w_up_hbm, w_up), (w_down_hbm, w_down)))
+    ]
+    for copy in shared:
+        copy.start()
+
+    f_keys.wait()
+
+    def turn_keys(r, carry):
+        keys_t[r] = keys[r].T
+        return carry
+
+    lax.fori_loop(0, ROWS, turn_keys, 0)
 
     def spread(tiles):
         r1[pl.ds(2 * plane, tiles)] = s1[pl.ds(2 * plane, tiles)]
@@ -241,7 +256,6 @@
     scale_inv = 1.0 / math.sqrt(HD)
     score_new = jnp.sum(query_rows.astype(F32) * key_new, axis=1, keepdims=True) * scale_inv
 
-    f_keys.wait()
     f_lengths.wait()
     f_values.wait()
     landed(recv_sem, 2, r3, N_DEV - 1)
@@ -252,9 +266,7 @@
     def attend(r, carry):
         own = pl.ds(r, H, stride=ROWS)
         q = jnp.concatenate([q_wide[0, own, :], q_wide[1, own, :]], axis=1).astype(BF16)
-        scores = (
-            lax.dot_general(q, keys[r], (((1,), (1,)), ((), ())), preferred_element_type=F32) * scale_inv
-        )
+        scores = jnp.dot(q, keys_t[r], preferred_element_type=F32) * scale_inv
         position = d * POS + lax.broadcasted_iota(jnp.int32, (H, POS), 1)
         valid = position < lengths[r]
         masked = jnp.where(valid, scores, NEG)
@@ -358,33 +370,30 @@
     tile = jnp.concatenate([pltpu.roll(gained_low, turn, 1), pltpu.roll(gained_high, turn, 1)], axis=0).astype(BF16)
     s6[...] = tile
     own = d * 2 + z_low
-    r6[core, own] = tile
+    r6[own] = tile
 
     def send_rows(n, carry):
-        send(5, s6, r6.at[core, own], *peer_all(n))
+        send(5, s6, r6.at[own], *peer_all(n))
         return carry
 
     lax.fori_loop(0, N_HALF - 1, send_rows, 0)
-    landed(recv_sem, 5, r6.at[0], N_HALF - 1)
-    forward = remote(6, r6.at[core], r6.at[core], sibling, d)
-    forward.start()
-    forward.wait_recv()
-
-    all_rows = N_POOL * ROWS
+    landed(recv_sem, 5, r6, N_HALF - 1)
+
+    some_rows = 2 * ROWS
 
     def assemble(g, sums):
         first = pl.multiple_of(g * 2 * GROUP, 2 * GROUP)
-        block = r6[:, pl.ds(first, 2 * GROUP)].astype(F32).reshape(2, GROUP, 2, 2, ROWS, LANES)
+        block = r6[pl.ds(first, 2 * GROUP)].astype(F32).reshape(GROUP, 2, 2, ROWS, LANES)
         chunks = [
-            (block[:, c, :, 0].reshape(all_rows, LANES), block[:, c, :, 1].reshape(all_rows, LANES))
+            (block[c, :, 0].reshape(some_rows, LANES), block[c, :, 1].reshape(some_rows, LANES))
             for c in range(GROUP)
         ]
         x_all[:, columns_of(g)] = jnp.concatenate(chunks_to_tiles(chunks), axis=1).astype(BF16)
         return tuple(total + chunk[1] for total, chunk in zip(sums, chunks))
 
-    zeros = jnp.zeros((all_rows, LANES), F32)
+    zeros = jnp.zeros((some_rows, LANES), F32)
     sums = lax.fori_loop(0, N_GROUP, assemble, (zeros,) * GROUP)
-    lane_all = lane_of((all_rows, LANES))
+    lane_all = lane_of((some_rows, LANES))
     squares_at = zeros
     for c in range(GROUP):
         at = (96 + c * (COLS % LANES)) % LANES
@@ -394,59 +403,41 @@
 
     f_gate.wait()
     f_up.wait()
+    shared[0].wait_recv()
+    shared[1].wait_recv()
     transposed = (((1,), (1,)), ((), ()))
-    gate = lax.dot_general(x_all[...], w_gate[...], transposed, preferred_element_type=F32) * norm
-    up = lax.dot_general(x_all[...], w_up[...], transposed, preferred_element_type=F32) * norm
+
+    def hidden_units(weights):
+        units = weights[...].reshape(2 * weights.shape[1], D)
+        return lax.dot_general(units, x_all[...], transposed, preferred_element_type=F32).T * norm
+
+    gate = hidden_units(w_gate)
+    up = hidden_units(w_up)
     activated = (gate / (1.0 + jnp.exp(-gate)) * up).astype(BF16)
 
     f_down.wait()
-
-    def give(i, carry):
-        g = group_at(i)
-        block = jnp.dot(activated, w_down[:, columns_of(g)], preferred_element_type=F32)
-        for c, (low_half, high_half) in enumerate(chunks_of(block)):
-            for q in range(N_POOL):
-                rows = slice(q * ROWS, (q + 1) * ROWS)
-                whole = jnp.concatenate([low_half[rows], high_half[rows]], axis=0)
-
-                @pl.when(core == q // 2)
-                def _():
-                    kept[g, 2 * c + q % 2] = whole
-
-                @pl.when(core != q // 2)
-                def _():
-                    t7[g, 2 * c + q % 2] = whole.astype(BF16)
-
-        pltpu.make_async_remote_copy(
-            src_ref=t7.at[g],
-            dst_ref=u7.at[g],
-            send_sem=send_sem.at[7],
-            recv_sem=pair_sem.at[g],
-            device_id=(sibling, d),
-            device_id_type=MESH,
-        ).start()
-        return carry
-
-    lax.fori_loop(0, N_GROUP, give, 0)
+    shared[2].wait_recv()
 
     def pass_on(i, carry):
         g = group_at(i)
-        pltpu.make_async_copy(u7.at[g], u7.at[g], pair_sem.at[g]).wait()
-        first = pl.multiple_of(g * 2 * GROUP, 2 * GROUP)
-        s7[pl.ds(first, 2 * GROUP)] = (kept[g] + u7[g].astype(F32)).astype(BF16)
-        for c in range(GROUP):
+        columns = columns_of(g)
+        weights = w_down[:, :, columns].reshape(2 * w_down.shape[1], GROUP_COLS)
+        block = jnp.dot(activated, weights, preferred_element_type=F32)
+        for c, (low_half, high_half) in enumerate(chunks_of(block)):
             for q in range(2):
-                at = first + 2 * c + q
+                rows = slice(q * ROWS, (q + 1) * ROWS)
+                at = (g * GROUP + c) * 2 + q
+                s7[at] = jnp.concatenate([low_half[rows], high_half[rows]], axis=0).astype(BF16)
 
                 @pl.when(at != own)
                 def _():
-                    send(8, s7.at[at], r7.at[own], q * 2 + core, g * GROUP + c)
+                    send(9, s7.at[at], r7.at[own], q * 2 + core, g * GROUP + c)
 
         return carry
 
     lax.fori_loop(0, N_GROUP, pass_on, 0)
     r7[own] = s7[own]
-    landed(recv_sem, 8, r7, N_HALF - 1)
+    landed(recv_sem, 9, r7, N_HALF - 1)
     ffn_low, ffn_high = unrotated(jnp.sum(r7[...].astype(F32), axis=0))
     out_ref[:, :LANES] = res_low + ffn_low
     out_ref[:, LANES:] = (res_high + ffn_high)[:, : COLS - LANES]
@@ -464,10 +455,10 @@
     landed(send_sem, 2, r3, N_DEV - 1)
     landed(send_sem, 3, r4, N_DEV - 1)
     landed(send_sem, 4, r5, N_DEV - 1)
-    landed(send_sem, 5, r6.at[0], N_HALF - 1)
-    forward.wait_send()
-    landed(send_sem, 7, t7, N_GROUP)
-    landed(send_sem, 8, r7, N_HALF - 1)
+    landed(send_sem, 5, r6, N_HALF - 1)
+    for copy in shared:
+        copy.wait_send()
+    landed(send_sem, 9, r7, N_HALF - 1)
 
 
 def local(
@@ -494,9 +485,9 @@
         like(cache_keys),
         like(cache_values),
         like(w_out),
-        pltpu.VMEM(w_gate.shape[::-1], BF16),
-        pltpu.VMEM(w_up.shape[::-1], BF16),
-        like(w_down),
+        pltpu.VMEM((2, *w_gate.shape[::-1]), BF16),
+        pltpu.VMEM((2, *w_up.shape[::-1]), BF16),
+        pltpu.VMEM((2, *w_down.shape), BF16),
         pltpu.VMEM((ROWS, 2 * LANES), F32),
         pltpu.VMEM((1, 2 * LANES), F32),
         pltpu.VMEM((2 * PLANE, ROWS, LANES), F32),
@@ -512,17 +503,14 @@
         pltpu.VMEM((N_DEV, *tile), BF16),
         pltpu.VMEM((N_DEV, *tile), BF16),
         pltpu.VMEM(tile, BF16),
-        pltpu.VMEM((2, N_HALF, *tile), BF16),
-        pltpu.VMEM((N_POOL * ROWS, D), BF16),
-        pltpu.VMEM((N_GROUP, 2 * GROUP, *tile), F32),
-        pltpu.VMEM((N_GROUP, 2 * GROUP, *tile), BF16),
-        pltpu.VMEM((N_GROUP, 2 * GROUP, *tile), BF16),
+        pltpu.VMEM((N_HALF, *tile), BF16),
+        pltpu.VMEM((2 * ROWS, D), BF16),
         pltpu.VMEM((N_HALF, *tile), BF16),
         pltpu.VMEM((N_HALF, *tile), BF16),
+        pltpu.VMEM((ROWS, HD, POS), BF16),
         pltpu.SemaphoreType.DMA((13,)),
-        pltpu.SemaphoreType.DMA((9,)),
-        pltpu.SemaphoreType.DMA((9,)),
-        pltpu.SemaphoreType.DMA((N_GROUP,)),
+        pltpu.SemaphoreType.DMA((10,)),
+        pltpu.SemaphoreType.DMA((10,)),
     ]
     return pl.pallas_call(
         kernel,

time: 62.7 us -> 57.8 us (0.922)
  Pallas kernels: 61.6 us -> 57.1 us
    pallas_call x1, Pallas kernels: 61.6 us -> 57.1 us  [local(): pl.pallas_call(kernel, out_shape=pltpu.VMEM(hidden_in.shape, F32), in_spe...]
where the time goes in v3:
time: 57.8 us; the launch traced here: 57.7 us
  Pallas kernels  57.1 us (99%)
  local copies, waits for them, and re-layouts  0.6 us (1%)
    pallas_call x1, Pallas kernels, local(): pl.pallas_call(kernel, out_shape=pltpu.VMEM(hidden_in.shape, F32), in_spe...  57.1 us

profile of v3, /device:TPU:0, one launch (start us, length us, event | category | flops | bytes accessed | tf_op | source)
XLA Modules:
  0.0 57.7 jit_solution(9778305997326870643)
XLA Ops:
  0.0 57.1 %shard_map.127 = f32[8,224]{1,0:T(8,128)S(1)} custom-call(bf16[8,224]{1,0:T(8,128)(2,1)} %hidden_hbm.1, f32[1,224]{1,0:T(1,128)} %bitcast.8, bf16[224,2560]{1,0:T(8,128)(2,1)} %w_latent_hbm.1, f32[1,2048]{1,0:T(1,128)} %bitcast.7, bf16[2048,512]{1,0:T(8,128)(2,1)} %w_query_hbm.1, bf16[8,512,256]{2,1,0:T(8,128)(2,1)} %keys_hbm.1, ...), custom_call_target="tpu_custom_call" | custom-call | tf_op jit(solution)/shard_map/pallas_call | solution.py:515
  57.1 0.6 %copy.15 = f32[8,224]{1,0:T(8,128)} copy(f32[8,224]{1,0:T(8,128)S(1)} %shard_map.127) | data formatting | bytes 14336

commit v4 on v3

--- a/solution.py
+++ b/solution.py
@@ -119,11 +119,15 @@
     barrier = pltpu.get_barrier_semaphore()
 
     def greet(n, carry):
-        pl.semaphore_signal(barrier, inc=1, device_id=peer_all(n), device_id_type=MESH)
-        return carry
-
-    lax.fori_loop(0, N_HALF - 1, greet, 0)
-    pl.semaphore_signal(barrier, inc=1, device_id=(sibling, d), device_id_type=MESH)
+        pl.semaphore_signal(barrier, inc=1, device_id=(p, peer(n, 0)), device_id_type=MESH)
+        return carry
+
+    lax.fori_loop(0, PLANE - 1, greet, 0)
+    across = 2 * (1 - z_low) + core
+    other = peer(PLANE - 1, 1)
+    column = ((p, other), (across, other), (across, d), (sibling, d))
+    for device in column:
+        pl.semaphore_signal(barrier, inc=1, device_id=device, device_id_type=MESH)
 
     f_q_gain = fetch(3, q_gain_hbm, q_gain_v)
     f_query = fetch(4, w_query_hbm, w_query)
@@ -174,7 +178,7 @@
         s1[2 * (c % PLANE) + c // PLANE] = part[:, c * LANES : (c + 1) * LANES]
     s1[2 * (EXTRA - 1) + 1] = jnp.broadcast_to(square_part, (ROWS, LANES))
 
-    pl.semaphore_wait(barrier, N_HALF)
+    pl.semaphore_wait(barrier, PLANE - 1 + len(column))
 
     def send_latent(n, carry):
         j = peer(n, 0)

time: 57.8 us -> 56.4 us (0.976)
  Pallas kernels: 57.1 us -> 55.7 us
    pallas_call x1, Pallas kernels: 57.1 us -> 55.7 us  [local(): pl.pallas_call(kernel, out_shape=pltpu.VMEM(hidden_in.shape, F32), in_spe...]
where the time goes in v4:
time: 56.4 us; the launch traced here: 56.3 us
  Pallas kernels  55.7 us (99%)
  local copies, waits for them, and re-layouts  0.6 us (1%)
    pallas_call x1, Pallas kernels, local(): pl.pallas_call(kernel, out_shape=pltpu.VMEM(hidden_in.shape, F32), in_spe...  55.7 us

profile of v4, /device:TPU:0, one launch (start us, length us, event | category | flops | bytes accessed | tf_op | source)
XLA Modules:
  0.0 56.3 jit_solution(14068881894194143412)
XLA Ops:
  0.0 55.7 %shard_map.127 = f32[8,224]{1,0:T(8,128)S(1)} custom-call(bf16[8,224]{1,0:T(8,128)(2,1)} %hidden_hbm.1, f32[1,224]{1,0:T(1,128)} %bitcast.8, bf16[224,2560]{1,0:T(8,128)(2,1)} %w_latent_hbm.1, f32[1,2048]{1,0:T(1,128)} %bitcast.7, bf16[2048,512]{1,0:T(8,128)(2,1)} %w_query_hbm.1, bf16[8,512,256]{2,1,0:T(8,128)(2,1)} %keys_hbm.1, ...), custom_call_target="tpu_custom_call" | custom-call | tf_op jit(solution)/shard_map/pallas_call | solution.py:519
  55.7 0.6 %copy.15 = f32[8,224]{1,0:T(8,128)} copy(f32[8,224]{1,0:T(8,128)S(1)} %shard_map.127) | data formatting | bytes 14336

commit v5 on v4

--- a/solution.py
+++ b/solution.py
@@ -21,7 +21,6 @@
 ROWS = 8
 COLS = 224
 LANES = 128
-CHUNKS = (QR + 2 * HD) // LANES + 1
 GROUP = 4
 GROUP_COLS = GROUP * COLS
 N_GROUP = N_DEV // GROUP
@@ -73,7 +72,8 @@
 FAR_GROUP_X = packed([2, 2, 1, 3, 1, 3, 0, 0], 2)
 FAR_GROUP_Y = packed([1, 0, 1, 1, 0, 0, 1, 0], 2)
 PLANE = 16
-EXTRA = CHUNKS - PLANE
+N_LINE = 4
+SCALE_INV = 1.0 / math.sqrt(HD)
 
 
 def entry(word, k):
@@ -85,8 +85,8 @@
     w_out_hbm, post_gain_hbm, w_gate_hbm, w_up_hbm, w_down_hbm,
     out_ref,
     hidden_v, in_gain_v, q_gain_v, post_gain_v, lengths, w_latent, w_query, keys, values, w_out, w_gate, w_up, w_down,
-    pad_hidden, pad_gain, s1, r1, s2, r2, s3, r3, q_wide, o_wide, s4, r4, s5, r5, s6, r6, x_all, s7, r7, keys_t,
-    local_sem, send_sem, recv_sem,
+    pad_hidden, pad_gain, s1, r1, s2, r2, s2_new, r2_new, s2_squares, r2_squares, sent_rows, s3, r3, q_wide, o_wide, s4, r4, s5, r5, s6, r6, x_all, s7, r7, keys_t,
+    local_sem, send_sem, recv_sem, wave_sem,
 ):
     p = lax.axis_index("pool")
     d = lax.axis_index("dev")
@@ -95,7 +95,6 @@
     z_high = lax.rem(d, 2)
     z_low = lax.div(p, 2)
     core = lax.rem(p, 2)
-    plane = lax.div(d, 2)
     sibling = z_low * 2 + 1 - core
 
     def peer(i, dz):
@@ -118,16 +117,20 @@
 
     barrier = pltpu.get_barrier_semaphore()
 
-    def greet(n, carry):
-        pl.semaphore_signal(barrier, inc=1, device_id=(p, peer(n, 0)), device_id_type=MESH)
-        return carry
-
-    lax.fori_loop(0, PLANE - 1, greet, 0)
+    def moved(dx, dy):
+        return lax.rem(x + dx, 4) * 8 + lax.rem(y + dy, 4) * 2 + z_high
+
     across = 2 * (1 - z_low) + core
     other = peer(PLANE - 1, 1)
-    column = ((p, other), (across, other), (across, d), (sibling, d))
-    for device in column:
-        pl.semaphore_signal(barrier, inc=1, device_id=device, device_id_type=MESH)
+    x_line = [(p, moved(step, 0)) for step in (2, 1, 3)]
+    y_line = [(p, moved(0, step)) for step in (2, 1, 3)]
+    z_column = [(p, other), (across, other), (across, d)]
+
+    def signal(semaphore, devices):
+        for device in devices:
+            pl.semaphore_signal(semaphore, inc=1, device_id=device, device_id_type=MESH)
+
+    signal(barrier, x_line + y_line + z_column + [(sibling, d)])
 
     f_q_gain = fetch(3, q_gain_hbm, q_gain_v)
     f_query = fetch(4, w_query_hbm, w_query)
@@ -174,27 +177,18 @@
     scaled_in = (hidden_f * in_gain_v[...]).astype(BF16)
     f_latent.wait()
     part = jnp.dot(scaled_in, w_latent[...], preferred_element_type=F32)
-    for c in range(CHUNKS - 1):
-        s1[2 * (c % PLANE) + c // PLANE] = part[:, c * LANES : (c + 1) * LANES]
-    s1[2 * (EXTRA - 1) + 1] = jnp.broadcast_to(square_part, (ROWS, LANES))
-
-    pl.semaphore_wait(barrier, PLANE - 1 + len(column))
-
-    def send_latent(n, carry):
-        j = peer(n, 0)
-        owner = lax.div(j, 2)
-
-        @pl.when(owner < EXTRA)
-        def _():
-            send(0, s1.at[pl.ds(2 * owner, 2)], r1.at[pl.ds(2 * plane, 2)], p, j)
-
-        @pl.when(owner >= EXTRA)
-        def _():
-            send(0, s1.at[pl.ds(2 * owner, 1)], r1.at[pl.ds(2 * plane, 1)], p, j)
-
-        return carry
-
-    lax.fori_loop(0, PLANE - 1, send_latent, 0)
+    coarse = square_part.astype(BF16).astype(F32)
+    squares_pair = jnp.where(lane_of((ROWS, LANES)) < LANES // 2, coarse, square_part - coarse)
+    for owner in range(N_LINE):
+        firsts = [4 * owner, 4 * owner + 1, 4 * owner + 2, 4 * owner + 3, QR // LANES + owner]
+        pieces = [part[:, c * LANES : (c + 1) * LANES] for c in firsts] + [squares_pair]
+        s1[owner] = jnp.concatenate(pieces, axis=0).astype(BF16)
+
+    pl.semaphore_wait(barrier, len(x_line + y_line + z_column) + 1)
+
+    for device in x_line:
+        send(0, s1.at[lax.div(device[1], 8)], r1.at[x], *device)
+    signal(wave_sem.at[0], z_column)
 
     shared = [
         remote(6 + k, source, target.at[1], sibling, d)
@@ -203,6 +197,33 @@
     for copy in shared:
         copy.start()
 
+    pl.semaphore_wait(wave_sem.at[0], len(z_column))
+    signal(wave_sem.at[1], x_line)
+
+    r1[x] = s1[x]
+    landed(recv_sem, 0, r1, N_LINE - 1)
+    line_sum = jnp.sum(r1[...].astype(F32), axis=0)
+    query_part = line_sum[: 4 * ROWS].astype(BF16)
+    s2[...] = query_part
+    r2[d] = query_part
+    s2_new[...] = line_sum[4 * ROWS :].astype(BF16)
+    r2_new[d] = line_sum[4 * ROWS :].astype(BF16)
+    pair_sum = line_sum[5 * ROWS :]
+    squares_line = pair_sum + pltpu.roll(pair_sum, LANES // 2, 1)
+    diagonal = lane_of((ROWS, LANES)) == lax.broadcasted_iota(jnp.int32, (ROWS, LANES), 0)
+    squares_row = jnp.sum(jnp.where(diagonal, squares_line, 0.0), axis=0, keepdims=True)
+    s2_squares[...] = squares_row
+    place = lax.rem(d, 8)
+    gives_squares = x == lax.rem(place, N_LINE)
+
+    pl.semaphore_wait(wave_sem.at[1], len(x_line))
+
+    @pl.when(gives_squares)
+    def _():
+        r2_squares[place] = squares_row
+        to_group(11, s2_squares, r2_squares.at[place])
+
+    to_group(1, s2, r2.at[d])
     f_keys.wait()
 
     def turn_keys(r, carry):
@@ -211,37 +232,27 @@
 
     lax.fori_loop(0, ROWS, turn_keys, 0)
 
-    def spread(tiles):
-        r1[pl.ds(2 * plane, tiles)] = s1[pl.ds(2 * plane, tiles)]
-        landed(recv_sem, 0, r1, (PLANE - 1) * tiles)
-        for t in range(tiles):
-            total = r1[t]
-            for source in range(1, PLANE):
-                total = total + r1[2 * source + t]
-            s2[t] = total
-            r2[2 * d + t] = total
-        to_group(1, s2.at[pl.ds(0, tiles)], r2.at[pl.ds(2 * d, tiles)])
-        landed(recv_sem, 1, r2, 2 * CHUNKS - tiles)
-
-    @pl.when(plane < EXTRA)
+    @pl.when(gives_squares)
     def _():
-        spread(2)
-
-    @pl.when(plane >= EXTRA)
+        landed(recv_sem, 11, r2_squares, 7)
+
+    @pl.when(jnp.logical_not(gives_squares))
     def _():
-        spread(1)
-
-    def summed_chunk(c):
-        at = 4 * (c % PLANE) + c // PLANE
-        return r2[at] + r2[at + 2]
-
-    row_scale = lax.rsqrt(summed_chunk(CHUNKS - 1) * (1.0 / D) + EPS)
-    latents = [summed_chunk(c) * row_scale for c in range(CHUNKS - 1)]
+        landed(recv_sem, 11, r2_squares, 8)
+
+    landed(recv_sem, 1, r2, N_DEV - 1)
+
+    squares_all = jnp.where(diagonal, jnp.sum(r2_squares[...], axis=0), 0.0)
+    row_scale = lax.rsqrt(jnp.sum(squares_all, axis=1, keepdims=True) * (1.0 / D) + EPS)
+    latents = []
+    for owner in range(N_LINE):
+        chunk = jnp.sum(r2[8 * owner : 8 * owner + 8].astype(F32), axis=0)
+        latents += [chunk[c * ROWS : (c + 1) * ROWS] * row_scale for c in range(4)]
     squares = latents[0] * latents[0]
     for c in range(1, QR // LANES):
         squares = squares + latents[c] * latents[c]
     latent_mean = jnp.sum(squares, axis=1, keepdims=True) * (1.0 / QR)
-    query_latent = jnp.concatenate(latents[: QR // LANES], axis=1)
+    query_latent = jnp.concatenate(latents, axis=1)
     f_q_gain.wait()
     query_normed = (query_latent * lax.rsqrt(latent_mean + EPS) * q_gain_v[...]).astype(BF16)
     f_query.wait()
@@ -251,14 +262,7 @@
     r3[d] = query_rows
     to_group(2, s3, r3.at[d])
 
-    def wide_new(first):
-        new = jnp.concatenate(latents[first : first + HD // LANES], axis=1).astype(BF16).astype(F32)
-        return jnp.concatenate([new, new], axis=0)
-
-    key_new = wide_new(QR // LANES)
-    value_new = wide_new((QR + HD) // LANES)
-    scale_inv = 1.0 / math.sqrt(HD)
-    score_new = jnp.sum(query_rows.astype(F32) * key_new, axis=1, keepdims=True) * scale_inv
+    to_group(10, s2_new, r2_new.at[d])
 
     f_lengths.wait()
     f_values.wait()
@@ -270,7 +274,7 @@
     def attend(r, carry):
         own = pl.ds(r, H, stride=ROWS)
         q = jnp.concatenate([q_wide[0, own, :], q_wide[1, own, :]], axis=1).astype(BF16)
-        scores = jnp.dot(q, keys_t[r], preferred_element_type=F32) * scale_inv
+        scores = jnp.dot(q, keys_t[r], preferred_element_type=F32) * SCALE_INV
         position = d * POS + lax.broadcasted_iota(jnp.int32, (H, POS), 1)
         valid = position < lengths[r]
         masked = jnp.where(valid, scores, NEG)
@@ -310,6 +314,21 @@
 
     lax.fori_loop(0, N_DEV, pack, 0)
     r4[d] = s4[d]
+
+    landed(recv_sem, 10, r2_new, N_DEV - 1)
+
+    def wide_new(first):
+        new = [
+            jnp.sum(r2_new[8 * owner : 8 * owner + 8, :ROWS].astype(F32), axis=0) * row_scale
+            for owner in (first, first + 1)
+        ]
+        new = jnp.concatenate(new, axis=1).astype(BF16).astype(F32)
+        return jnp.concatenate([new, new], axis=0)
+
+    key_new = wide_new(0)
+    value_new = wide_new(2)
+    score_new = jnp.sum(query_rows.astype(F32) * key_new, axis=1, keepdims=True) * SCALE_INV
+
     landed(recv_sem, 3, r4, N_DEV - 1)
 
     pieces = r4[:, :, HD:].astype(F32)
@@ -446,16 +465,13 @@
     out_ref[:, :LANES] = res_low + ffn_low
     out_ref[:, LANES:] = (res_high + ffn_high)[:, : COLS - LANES]
 
-    @pl.when(plane < EXTRA)
+    @pl.when(gives_squares)
     def _():
-        landed(send_sem, 0, s1, PLANE - 1 + EXTRA - 1)
-        landed(send_sem, 1, r2, 2 * (N_DEV - 1))
-
-    @pl.when(plane >= EXTRA)
-    def _():
-        landed(send_sem, 0, s1, PLANE - 1 + EXTRA)
-        landed(send_sem, 1, r2, N_DEV - 1)
-
+        landed(send_sem, 11, sent_rows, N_DEV - 1)
+
+    landed(send_sem, 0, r1, N_LINE - 1)
+    landed(send_sem, 1, r2, N_DEV - 1)
+    landed(send_sem, 10, r2_new, N_DEV - 1)
     landed(send_sem, 2, r3, N_DEV - 1)
     landed(send_sem, 3, r4, N_DEV - 1)
     landed(send_sem, 4, r5, N_DEV - 1)
@@ -494,10 +510,15 @@
         pltpu.VMEM((2, *w_down.shape), BF16),
         pltpu.VMEM((ROWS, 2 * LANES), F32),
         pltpu.VMEM((1, 2 * LANES), F32),
-        pltpu.VMEM((2 * PLANE, ROWS, LANES), F32),
-        pltpu.VMEM((2 * PLANE, ROWS, LANES), F32),
-        pltpu.VMEM((2, ROWS, LANES), F32),
-        pltpu.VMEM((2 * N_DEV, ROWS, LANES), F32),
+        pltpu.VMEM((N_LINE, 6 * ROWS, LANES), BF16),
+        pltpu.VMEM((N_LINE, 6 * ROWS, LANES), BF16),
+        pltpu.VMEM((4 * ROWS, LANES), BF16),
+        pltpu.VMEM((N_DEV, 4 * ROWS, LANES), BF16),
+        pltpu.VMEM(tile, BF16),
+        pltpu.VMEM((N_DEV, *tile), BF16),
+        pltpu.VMEM((1, LANES), F32),
+        pltpu.VMEM((8, 1, LANES), F32),
+        pltpu.VMEM((N_DEV, 1, LANES), F32),
         pltpu.VMEM((2 * ROWS, HD), BF16),
         pltpu.VMEM((N_DEV, 2 * ROWS, HD), BF16),
         pltpu.VMEM((HD // LANES, H * ROWS, LANES), F32),
@@ -513,8 +534,9 @@
         pltpu.VMEM((N_HALF, *tile), BF16),
         pltpu.VMEM((ROWS, HD, POS), BF16),
         pltpu.SemaphoreType.DMA((13,)),
-        pltpu.SemaphoreType.DMA((10,)),
-        pltpu.SemaphoreType.DMA((10,)),
+        pltpu.SemaphoreType.DMA((12,)),
+        pltpu.SemaphoreType.DMA((12,)),
+        pltpu.SemaphoreType.REGULAR((2,)),
     ]
     return pl.pallas_call(
         kernel,

time: 56.4 us -> 54.8 us (0.972)
  Pallas kernels: 55.7 us -> 54.1 us
    pallas_call x1, Pallas kernels: 55.7 us -> 54.1 us  [local(): pl.pallas_call(kernel, out_shape=pltpu.VMEM(hidden_in.shape, F32), in_spe...]
where the time goes in v5:
time: 54.8 us; the launch traced here: 54.7 us
  Pallas kernels  54.1 us (99%)
  local copies, waits for them, and re-layouts  0.6 us (1%)
    pallas_call x1, Pallas kernels, local(): pl.pallas_call(kernel, out_shape=pltpu.VMEM(hidden_in.shape, F32), in_spe...  54.1 us

profile of v5, /device:TPU:0, one launch (start us, length us, event | category | flops | bytes accessed | tf_op | source)
XLA Modules:
  0.0 54.7 jit_solution(15011474034329532795)
XLA Ops:
  0.0 54.1 %shard_map.127 = f32[8,224]{1,0:T(8,128)S(1)} custom-call(bf16[8,224]{1,0:T(8,128)(2,1)} %hidden_hbm.1, f32[1,224]{1,0:T(1,128)} %bitcast.8, bf16[224,2560]{1,0:T(8,128)(2,1)} %w_latent_hbm.1, f32[1,2048]{1,0:T(1,128)} %bitcast.7, bf16[2048,512]{1,0:T(8,128)(2,1)} %w_query_hbm.1, bf16[8,512,256]{2,1,0:T(8,128)(2,1)} %keys_hbm.1, ...), custom_call_target="tpu_custom_call" | custom-call | tf_op jit(solution)/shard_map/pallas_call | solution.py:541
  54.1 0.6 %copy.15 = f32[8,224]{1,0:T(8,128)} copy(f32[8,224]{1,0:T(8,128)S(1)} %shard_map.127) | data formatting | bytes 14336

commit v6 on v5

--- a/solution.py
+++ b/solution.py
@@ -85,7 +85,7 @@
     w_out_hbm, post_gain_hbm, w_gate_hbm, w_up_hbm, w_down_hbm,
     out_ref,
     hidden_v, in_gain_v, q_gain_v, post_gain_v, lengths, w_latent, w_query, keys, values, w_out, w_gate, w_up, w_down,
-    pad_hidden, pad_gain, s1, r1, s2, r2, s2_new, r2_new, s2_squares, r2_squares, sent_rows, s3, r3, q_wide, o_wide, s4, r4, s5, r5, s6, r6, x_all, s7, r7, keys_t,
+    pad_hidden, pad_gain, s1, r1, s2, r2, s2_new, r2_new, s3_new, r3_new, s2_squares, r2_squares, sent_rows, s3, r3, q_wide, o_wide, s4, r4, s4_mass, r4_mass, s5, r5, s6, r6, x_all, s7, r7, keys_t,
     local_sem, send_sem, recv_sem, wave_sem,
 ):
     p = lax.axis_index("pool")
@@ -165,7 +165,7 @@
             send(i, source, target, p, peer(lax.rem(n, 16), 1 - lax.div(n, 16)))
             return carry
 
-        lax.fori_loop(0, N_DEV - 1, step, 0)
+        lax.fori_loop(0, N_DEV - 1, step, 0, unroll=31)
 
     pad_hidden[...] = jnp.zeros_like(pad_hidden)
     pad_gain[...] = jnp.zeros_like(pad_gain)
@@ -207,13 +207,13 @@
     s2[...] = query_part
     r2[d] = query_part
     s2_new[...] = line_sum[4 * ROWS :].astype(BF16)
-    r2_new[d] = line_sum[4 * ROWS :].astype(BF16)
     pair_sum = line_sum[5 * ROWS :]
     squares_line = pair_sum + pltpu.roll(pair_sum, LANES // 2, 1)
     diagonal = lane_of((ROWS, LANES)) == lax.broadcasted_iota(jnp.int32, (ROWS, LANES), 0)
     squares_row = jnp.sum(jnp.where(diagonal, squares_line, 0.0), axis=0, keepdims=True)
     s2_squares[...] = squares_row
     place = lax.rem(d, 8)
+    adds_new = place == 2 * x
     gives_squares = x == lax.rem(place, N_LINE)
 
     pl.semaphore_wait(wave_sem.at[1], len(x_line))
@@ -224,6 +224,15 @@
         to_group(11, s2_squares, r2_squares.at[place])
 
     to_group(1, s2, r2.at[d])
+
+    @pl.when(adds_new)
+    def _():
+        r2_new[place] = s2_new[...]
+
+    @pl.when(jnp.logical_not(adds_new))
+    def _():
+        send(10, s2_new, r2_new.at[place], p, x * 8 + 2 * x)
+
     f_keys.wait()
 
     def turn_keys(r, carry):
@@ -262,7 +271,15 @@
     r3[d] = query_rows
     to_group(2, s3, r3.at[d])
 
-    to_group(10, s2_new, r2_new.at[d])
+    @pl.when(adds_new)
+    def _():
+        landed(recv_sem, 10, r2_new, 7)
+        total = jnp.sum(r2_new[...].astype(F32), axis=0)[:ROWS]
+        coarse = total.astype(BF16).astype(F32)
+        both = jnp.concatenate([coarse, total - coarse], axis=0).astype(BF16)
+        s3_new[...] = both
+        r3_new[x] = both
+        to_group(13, s3_new, r3_new.at[x])
 
     f_lengths.wait()
     f_values.wait()
@@ -293,35 +310,39 @@
 
     lax.fori_loop(0, ROWS, attend, 0, unroll=UNROLL)
 
+    pair_shape = (2 * ROWS, LANES)
+    diagonal_pair = lane_of(pair_shape) == lax.broadcasted_iota(jnp.int32, pair_shape, 0)
+
     def pack(n, carry):
         j = peer(lax.rem(n, 16), 1 - lax.div(n, 16))
         rows = pl.ds(pl.multiple_of(j * 2 * ROWS, 2 * ROWS), 2 * ROWS)
         s4[j, :, :LANES] = o_wide[0, rows, :].astype(BF16)
-        s4[j, :, LANES:HD] = o_wide[1, rows, :].astype(BF16)
+        s4[j, :, LANES:] = o_wide[1, rows, :].astype(BF16)
         log_mass = o_wide[2, rows, :]
-        high = log_mass.astype(BF16).astype(F32)
-        rest = log_mass - high
-        middle = rest.astype(BF16).astype(F32)
-        low = rest - middle
-        lane = lane_of(log_mass.shape)
-        s4[j, :, HD:] = jnp.where(lane == 0, high, jnp.where(lane == 1, middle, low)).astype(BF16)
+        s4_mass[j] = jnp.sum(jnp.where(diagonal_pair, log_mass, 0.0), axis=0, keepdims=True)
 
         @pl.when(n < N_DEV - 1)
         def _():
             send(3, s4.at[j], r4.at[d], p, j)
+            send(12, s4_mass.at[j], r4_mass.at[d], p, j)
 
         return carry
 
     lax.fori_loop(0, N_DEV, pack, 0)
     r4[d] = s4[d]
-
-    landed(recv_sem, 10, r2_new, N_DEV - 1)
+    r4_mass[d] = s4_mass[d]
+
+    @pl.when(adds_new)
+    def _():
+        landed(recv_sem, 13, r3_new, N_LINE - 1)
+
+    @pl.when(jnp.logical_not(adds_new))
+    def _():
+        landed(recv_sem, 13, r3_new, N_LINE)
 
     def wide_new(first):
-        new = [
-            jnp.sum(r2_new[8 * owner : 8 * owner + 8, :ROWS].astype(F32), axis=0) * row_scale
-            for owner in (first, first + 1)
-        ]
+        pieces = [r3_new[owner].astype(F32) for owner in (first, first + 1)]
+        new = [(piece[:ROWS] + piece[ROWS:]) * row_scale for piece in pieces]
         new = jnp.concatenate(new, axis=1).astype(BF16).astype(F32)
         return jnp.concatenate([new, new], axis=0)
 
@@ -331,13 +352,14 @@
 
     landed(recv_sem, 3, r4, N_DEV - 1)
 
-    pieces = r4[:, :, HD:].astype(F32)
-    log_all = jnp.sum(jnp.where(lane_of(pieces.shape) < 3, pieces, 0.0), axis=2, keepdims=True)
+    landed(recv_sem, 12, r4_mass, N_DEV - 1)
+    masses = jnp.broadcast_to(r4_mass[...], (N_DEV, *pair_shape))
+    log_all = jnp.sum(jnp.where(diagonal_pair[None], masses, 0.0), axis=2, keepdims=True)
     top_all = jnp.maximum(jnp.max(log_all, axis=0), score_new)
     share = jnp.exp(log_all - top_all[None])
     fresh = jnp.exp(score_new - top_all)
     mass_all = jnp.sum(share, axis=0) + fresh
-    numerator = jnp.sum(share * r4[:, :, :HD].astype(F32), axis=0)
+    numerator = jnp.sum(share * r4[...].astype(F32), axis=0)
     numerator = numerator + fresh.astype(BF16).astype(F32) * value_new
     attended = numerator / mass_all
     own_heads = jnp.concatenate([attended[:ROWS], attended[ROWS:]], axis=1).astype(BF16)
@@ -399,7 +421,7 @@
         send(5, s6, r6.at[own], *peer_all(n))
         return carry
 
-    lax.fori_loop(0, N_HALF - 1, send_rows, 0)
+    lax.fori_loop(0, N_HALF - 1, send_rows, 0, unroll=21)
     landed(recv_sem, 5, r6, N_HALF - 1)
 
     some_rows = 2 * ROWS
@@ -460,10 +482,6 @@
 
     lax.fori_loop(0, N_GROUP, pass_on, 0)
     r7[own] = s7[own]
-    landed(recv_sem, 9, r7, N_HALF - 1)
-    ffn_low, ffn_high = unrotated(jnp.sum(r7[...].astype(F32), axis=0))
-    out_ref[:, :LANES] = res_low + ffn_low
-    out_ref[:, LANES:] = (res_high + ffn_high)[:, : COLS - LANES]
 
     @pl.when(gives_squares)
     def _():
@@ -471,13 +489,28 @@
 
     landed(send_sem, 0, r1, N_LINE - 1)
     landed(send_sem, 1, r2, N_DEV - 1)
-    landed(send_sem, 10, r2_new, N_DEV - 1)
+
+    @pl.when(adds_new)
+    def _():
+        landed(send_sem, 13, r5, N_DEV - 1)
+
+    @pl.when(jnp.logical_not(adds_new))
+    def _():
+        landed(send_sem, 10, r2_new, 1)
+
     landed(send_sem, 2, r3, N_DEV - 1)
     landed(send_sem, 3, r4, N_DEV - 1)
     landed(send_sem, 4, r5, N_DEV - 1)
     landed(send_sem, 5, r6, N_HALF - 1)
     for copy in shared:
         copy.wait_send()
+    landed(send_sem, 12, r4_mass, N_DEV - 1)
+
+    landed(recv_sem, 9, r7, N_HALF - 1)
+    ffn_low, ffn_high = unrotated(jnp.sum(r7[...].astype(F32), axis=0))
+    out_ref[:, :LANES] = res_low + ffn_low
+    out_ref[:, LANES:] = (res_high + ffn_high)[:, : COLS - LANES]
+
     landed(send_sem, 9, r7, N_HALF - 1)
 
 
@@ -515,7 +548,9 @@
         pltpu.VMEM((4 * ROWS, LANES), BF16),
         pltpu.VMEM((N_DEV, 4 * ROWS, LANES), BF16),
         pltpu.VMEM(tile, BF16),
-        pltpu.VMEM((N_DEV, *tile), BF16),
+        pltpu.VMEM((8, *tile), BF16),
+        pltpu.VMEM(tile, BF16),
+        pltpu.VMEM((N_LINE, *tile), BF16),
         pltpu.VMEM((1, LANES), F32),
         pltpu.VMEM((8, 1, LANES), F32),
         pltpu.VMEM((N_DEV, 1, LANES), F32),
@@ -523,8 +558,10 @@
         pltpu.VMEM((N_DEV, 2 * ROWS, HD), BF16),
         pltpu.VMEM((HD // LANES, H * ROWS, LANES), F32),
         pltpu.VMEM((MSG // LANES, H * ROWS, LANES), F32),
-        pltpu.VMEM((N_DEV, 2 * ROWS, MSG), BF16),
-        pltpu.VMEM((N_DEV, 2 * ROWS, MSG), BF16),
+        pltpu.VMEM((N_DEV, 2 * ROWS, HD), BF16),
+        pltpu.VMEM((N_DEV, 2 * ROWS, HD), BF16),
+        pltpu.VMEM((N_DEV, 1, LANES), F32),
+        pltpu.VMEM((N_DEV, 1, LANES), F32),
         pltpu.VMEM((N_DEV, *tile), BF16),
         pltpu.VMEM((N_DEV, *tile), BF16),
         pltpu.VMEM(tile, BF16),
@@ -533,9 +570,9 @@
         pltpu.VMEM((N_HALF, *tile), BF16),
         pltpu.VMEM((N_HALF, *tile), BF16),
         pltpu.VMEM((ROWS, HD, POS), BF16),
-        pltpu.SemaphoreType.DMA((13,)),
-        pltpu.SemaphoreType.DMA((12,)),
-        pltpu.SemaphoreType.DMA((12,)),
+        pltpu.SemaphoreType.DMA((14,)),
+        pltpu.SemaphoreType.DMA((14,)),
+        pltpu.SemaphoreType.DMA((14,)),
         pltpu.SemaphoreType.REGULAR((2,)),
     ]
     return pl.pallas_call(

time: 54.8 us -> 54 us (0.985)
  Pallas kernels: 54.1 us -> 53.3 us
    pallas_call x1, Pallas kernels: 54.1 us -> 53.3 us  [local(): pl.pallas_call(kernel, out_shape=pltpu.VMEM(hidden_in.shape, F32), in_spe...]
where the time goes in v6:
time: 54 us; the launch traced here: 53.9 us
  Pallas kernels  53.3 us (99%)
  local copies, waits for them, and re-layouts  0.6 us (1%)
    pallas_call x1, Pallas kernels, local(): pl.pallas_call(kernel, out_shape=pltpu.VMEM(hidden_in.shape, F32), in_spe...  53.3 us

profile of v6, /device:TPU:0, one launch (start us, length us, event | category | flops | bytes accessed | tf_op | source)
XLA Modules:
  0.0 53.9 jit_solution(4395471283933290189)
XLA Ops:
  0.0 53.3 %shard_map.127 = f32[8,224]{1,0:T(8,128)S(1)} custom-call(bf16[8,224]{1,0:T(8,128)(2,1)} %hidden_hbm.1, f32[1,224]{1,0:T(1,128)} %bitcast.8, bf16[224,2560]{1,0:T(8,128)(2,1)} %w_latent_hbm.1, f32[1,2048]{1,0:T(1,128)} %bitcast.7, bf16[2048,512]{1,0:T(8,128)(2,1)} %w_query_hbm.1, bf16[8,512,256]{2,1,0:T(8,128)(2,1)} %keys_hbm.1, ...), custom_call_target="tpu_custom_call" | custom-call | tf_op jit(solution)/shard_map/pallas_call | solution.py:578
  53.3 0.6 %copy.15 = f32[8,224]{1,0:T(8,128)} copy(f32[8,224]{1,0:T(8,128)S(1)} %shard_map.127) | data formatting | bytes 14336
